TPU v7x, 32 devices: a whole 2x2x4 slice. The times are simulated.
32 devices in a mesh: groups: 2 (over y), gx: 4 (over x, core), gy: 4 (over z).
Axes of the slice: x: 2, y: 2, z: 4, core: 2. Of those that a mesh axis runs over, the one named last changes fastest.
Arguments:
- tokens: bfloat16 [2, 1024, 18432], P(None, 'groups', ('gx', 'gy')), parts along dimension 1, may hold values from -400 to 400
- norm_gain: bfloat16 [18432], P(('gx', 'gy')), may hold values from 0.5 to 1.5
- gate_weight: bfloat16 [18432, 9216], P('gx', 'gy'), may hold values from -0.046875 to 0.046875
- up_weight: bfloat16 [18432, 9216], P('gx', 'gy'), may hold values from -0.046875 to 0.046875
- down_weight: bfloat16 [9216, 18432], P('gy', 'gx'), may hold values from -0.09375 to 0.09375
Outputs:
- ffn_output: bfloat16 [2, 1024, 18432], P(None, 'groups', ('gx', 'gy')), parts along dimension 1
There are 2 independent parts, one for each index of `groups`. A program takes and returns all parts, laid end to end along the dimension named above; an argument that names none is the same for every part. Nothing has to cross between parts.
All inputs are finite; a program needn't handle non-finite values.
Results may differ from a plain program's by a relative error of at most 0.0065.
Values may be sent and summed in bfloat16 or wider, within the bound.
No kernel may reach another device: no remote copies, remote signals or barrier semaphores. Data moves between devices by JAX's collectives and lax.ppermute only.
A program may use at most 192 MiB of HBM per device.

v0:
```python
import jax
import jax.numpy as jnp
from jax import lax
from jax.sharding import PartitionSpec as P

D = 18432


epsilon = 1e-05


def layer_block(rows_in, norm_gain, gate_weight, up_weight, down_weight):
    values = rows_in.astype(jnp.float32)
    squares = lax.psum(jnp.sum(values * values, axis=1), ("gx", "gy"))
    normed = (
        values * lax.rsqrt(squares / D + epsilon)[:, None] * norm_gain.astype(jnp.float32)[None, :]
    ).astype(jnp.bfloat16)
    shard_piece = lax.all_gather(normed, "gy", axis=1, tiled=True)
    gate_sum = jnp.dot(shard_piece, gate_weight, preferred_element_type=jnp.float32)
    up_sum = jnp.dot(shard_piece, up_weight, preferred_element_type=jnp.float32)
    gate_share, up_share = (
        lax.psum_scatter(gate_sum, "gx", scatter_dimension=1, tiled=True),
        lax.psum_scatter(up_sum, "gx", scatter_dimension=1, tiled=True),
    )
    hidden = (jax.nn.silu(gate_share) * up_share).astype(jnp.bfloat16)
    terms = jnp.dot(
        lax.all_gather(hidden, "gx", axis=1, tiled=True),
        down_weight,
        preferred_element_type=jnp.float32,
    )
    return lax.psum_scatter(terms, "gy", scatter_dimension=1, tiled=True).astype(jnp.bfloat16)


def local(tokens, norm_gain, gate_weight, up_weight, down_weight):
    micro_count, row_count, width = tokens.shape
    merged = layer_block(
        tokens.reshape(micro_count * row_count, width),
        norm_gain,
        gate_weight,
        up_weight,
        down_weight,
    )
    return merged.reshape(micro_count, row_count, merged.shape[1])


def solution(mesh):
    in_specs = (
        P(None, "groups", ("gx", "gy")),
        P(("gx", "gy")),
        P("gx", "gy"),
        P("gx", "gy"),
        P("gy", "gx"),
    )
    out_specs = P(None, "groups", ("gx", "gy"))
    return jax.shard_map(local, mesh=mesh, in_specs=in_specs, out_specs=out_specs, check_vma=False)
```

profile of v0, /device:TPU:0, one launch (start us, length us, event | category | flops | bytes accessed | tf_op | source)
XLA Modules:
  0.0 795.8 jit_solution(4736648084970979163)
XLA Ops:
  6.5 0.0 all-gather.3.cloned.1.call-start
  6.5 2.2 multiply_reduce_fusion
  8.7 35.1 %psum.7 = f32[1024]{0:T(1024)S(1)} all-reduce(f32[1024]{0:T(1024)S(1)} %bitcast.16), channel_id=1, replica_groups=mesh['groups'=2,'gx'=4,'gy'=4] {'gx','gy'}, use_global_device_ids=true, to_apply=%region_1.0 | all-reduce | flops 1024 | bytes 8192 | tf_op jit(solution)/shard_map/psum | solution.py:14
  43.9 0.7 convert_element_type.24
  44.6 3.7 fusion.1
  48.3 0.0 all-gather.3.cloned.1.call-update
  48.3 0.0 reduce-scatter.4.cloned.1.call-start
  48.4 164.1 %all-gather.3.cloned.1.call-done = bf16[1024,4608]{1,0:T(8,128)(2,1)} async-done(((bf16[1024,1152]{1,0:T(8,128)(2,1)}), bf16[1024,4608]{1,0:T(8,128)(2,1)}) %all-gather.3.cloned.1.call-update) | async-done | bytes 9437200 | tf_op jit(solution)/shard_map/all_gather | solution.py:18
  212.5 30.2 %fusion.2 = f32[1024,2304]{0,1:T(8,128)} fusion(bf16[1024,4608]{1,0:T(8,128)(2,1)} %all-gather.3.cloned.1.call-done, bf16[4608,2304]{1,0:T(8,128)(2,1)} %param.7), kind=kOutput, calls=%fused_computation.6 | convolution fusion | flops 21743271936 | bytes 40108032 | tf_op jit(solution)/shard_map/dot_general | solution.py:19
  242.7 0.0 reduce-scatter.4.cloned.1.call-update
  242.7 0.2 reduce-scatter.6.cloned.1.call-start
  243.0 30.9 %fusion.3 = f32[1024,2304]{0,1:T(8,128)} fusion(bf16[1024,4608]{1,0:T(8,128)(2,1)} %all-gather.3.cloned.1.call-done, bf16[4608,2304]{1,0:T(8,128)(2,1)} %param.8), kind=kOutput, calls=%fused_computation.7 | convolution fusion | flops 21743271936 | bytes 40108032 | tf_op jit(solution)/shard_map/dot_general | solution.py:20
  273.8 0.0 reduce-scatter.6.cloned.1.call-update
  273.9 0.0 all-gather.5.cloned.1.call-start
  273.9 45.6 %reduce-scatter.4.cloned.1.call-done = f32[1024,576]{0,1:T(8,128)} async-done(((f32[1024,2304]{0,1:T(8,128)}), f32[1024,576]{0,1:T(8,128)}) %reduce-scatter.4.cloned.1.call-update) | async-done | bytes 2359312 | tf_op jit(solution)/shard_map/reduce_scatter | solution.py:22
  319.5 81.1 %reduce-scatter.6.cloned.1.call-done = f32[1024,576]{0,1:T(8,128)} async-done(((f32[1024,2304]{0,1:T(8,128)}), f32[1024,576]{0,1:T(8,128)}) %reduce-scatter.6.cloned.1.call-update) | async-done | bytes 2359312 | tf_op jit(solution)/shard_map/reduce_scatter | solution.py:23
  400.6 4.1 multiply_convert_fusion
  404.7 0.0 all-gather.5.cloned.1.call-update
  404.7 0.3 reduce-scatter.8.cloned.1.call-start
  405.0 37.3 %all-gather.5.cloned.1.call-done = bf16[1024,2304]{0,1:T(8,128)(2,1)} async-done(((bf16[1024,576]{0,1:T(8,128)(2,1)}), bf16[1024,2304]{0,1:T(8,128)(2,1)}) %all-gather.5.cloned.1.call-update) | async-done | bytes 4718608 | tf_op jit(solution)/shard_map/all_gather | solution.py:27
  442.3 29.0 %fusion.4 = f32[1024,4608]{1,0:T(8,128)} fusion(bf16[1024,2304]{0,1:T(8,128)(2,1)} %all-gather.5.cloned.1.call-done, bf16[2304,4608]{1,0:T(8,128)(2,1)} %param.9), kind=kOutput, calls=%fused_computation.8 | convolution fusion | flops 21743271936 | bytes 44826624 | tf_op jit(solution)/shard_map/dot_general | solution.py:26
  471.3 0.0 reduce-scatter.8.cloned.1.call-update
  471.3 313.9 %reduce-scatter.8.cloned.1.call-done = f32[1024,1152]{1,0:T(8,128)} async-done(((f32[1024,4608]{1,0:T(8,128)}), f32[1024,1152]{1,0:T(8,128)}) %reduce-scatter.8.cloned.1.call-update) | async-done | bytes 4718608 | tf_op jit(solution)/shard_map/reduce_scatter | solution.py:31
  785.3 4.0 convert_element_type.27
  (2 shorter events, 0.0 us)
Async XLA Ops:
  6.5 206.0 %all-gather.3.cloned.1.call-start = ((), (), s32[]{:S(2)}) async-start(), calls=%async_computation.3 | async-start | bytes 11796480 | tf_op jit(solution)/shard_map/all_gather | solution.py:18
  48.3 271.2 %reduce-scatter.4.cloned.1.call-start = ((), (), s32[]{:S(2)}) async-start(), calls=%async_computation.4 | async-start | bytes 11796480 | tf_op jit(solution)/shard_map/reduce_scatter | solution.py:22
  242.7 157.9 %reduce-scatter.6.cloned.1.call-start = ((), (), s32[]{:S(2)}) async-start(), calls=%async_computation.5 | async-start | bytes 11796480 | tf_op jit(solution)/shard_map/reduce_scatter | solution.py:23
  273.9 168.5 %all-gather.5.cloned.1.call-start = ((), (), s32[]{:S(2)}) async-start(), calls=%async_computation.6 | async-start | bytes 5898240 | tf_op jit(solution)/shard_map/all_gather | solution.py:27
  404.7 380.6 %reduce-scatter.8.cloned.1.call-start = ((), (), s32[]{:S(2)}) async-start(), calls=%async_computation.7 | async-start | bytes 23592960 | tf_op jit(solution)/shard_map/reduce_scatter | solution.py:31
Sparse Core Ops, SparseCore 0:
  48.4 164.0 all-gather.2
  242.9 76.6 reduce-scatter.3
  322.1 78.4 reduce-scatter.5
  404.8 37.4 all-gather.4
  471.4 313.7 reduce-scatter.7
where the time goes:
time: 796 us
  waiting for transfers between devices  642 us (81%)
  matrix products  90.1 us (11%)
  blocking collectives  35.1 us (4%)
  other arithmetic  14.7 us (2%)
  between operations  13.1 us (2%)
    reduce_scatter x1, waiting for transfers between devices, layer_block(): lax.psum_scatter(terms, 'gy', scatter_dimension=1, tiled=True)  314 us
    all_gather x1, waiting for transfers between devices, layer_block(): shard_piece = lax.all_gather(normed, 'gy', axis=1, tiled=True)  164 us
    reduce_scatter x1, waiting for transfers between devices, layer_block(): lax.psum_scatter(up_sum, 'gx', scatter_dimension=1, tiled=True)  81.1 us
    reduce_scatter x1, waiting for transfers between devices, layer_block(): lax.psum_scatter(gate_sum, 'gx', scatter_dimension=1, tiled=True)  45.6 us
    all_gather x1, waiting for transfers between devices, layer_block(): lax.all_gather(hidden, 'gx', axis=1, tiled=True)  37.3 us
    psum x1, blocking collectives, layer_block(): squares = lax.psum(jnp.sum(values * values, axis=1), ('gx', 'gy'))  35.1 us
    dot_general x1, matrix products, layer_block(): up_sum = jnp.dot(shard_piece, up_weight, preferred_element_type=jnp.float32)  30.9 us
    dot_general x1, matrix products, layer_block(): jnp.dot(shard_piece, gate_weight, preferred_element_type=jnp.float32)  30.2 us
  transfers between devices with their start and end apart: 5, of which 5 were waited for; matrix products, arithmetic and copies ran while one was open for 4% of the time, Pallas kernels for 0%

commit v1 on v0

v1 whole, which is shorter than its diff:
```python
import functools

import jax
import jax.numpy as jnp
from jax import lax
from jax.experimental import pallas as pl
from jax.experimental.pallas import tpu as pltpu
from jax.sharding import PartitionSpec as P

D = 18432
CORES = 2
CHUNKS = (256, 256, 256, 256)
ORDER = (1, 1, 3, 1, 2, 0, 3, 0, 1, 0, 2, 1, 0, 3, 0, 2, 1, 3, 0, 1, 3, 1, 2, 3, 1, 2, 3, 0, 3, 2, 1, 2, 2, 1, 3, 2, 0, 3, 2, 3, 2)
VMEM = 48 * 1024 * 1024
bf16, f32 = jnp.bfloat16, jnp.float32


epsilon = 1e-05


def rotate(value, axis, count, stride, by):
    pairs = []
    for place in range(count):
        for rest in range(stride):
            pairs.append((place * stride + rest, (place + by) % count * stride + rest))
    return lax.ppermute(value, axis, pairs)


def swap_core(value, size):
    return lax.ppermute(value, "gx", [(i, i ^ 1) for i in range(size)])


def gate_up_kernel(n, first, at, *refs):
    own, up, down = refs[0], refs[1:n], refs[n : 2 * n - 1]
    scale, gain, gate_w, up_w, send_gate, send_up, keep, normed, product = refs[2 * n - 1 :]
    place, core = at[0], at[1]
    width = own.shape[1]
    rows = slice(first, first + own.shape[0])
    half = product.shape[0] // CORES

    @pl.when(pl.program_id(0) == 0)
    def _():
        def fill(t, source):
            column = pl.multiple_of(lax.rem(place + (n - t), n) * width, 128)
            values = source[...].astype(f32) * scale[rows, :] * gain[t : t + 1, :]
            normed[:, pl.ds(column, width)] = values.astype(bf16)

        fill(0, own)
        for t in range(1, n):
            pl.when(place >= t)(functools.partial(fill, t, up[t - 1]))
            pl.when(place < t)(functools.partial(fill, t, down[n - t - 1]))

    for k, (weight, send) in enumerate(((gate_w, send_gate), (up_w, send_up))):
        product[...] = jnp.dot(normed[...], weight[...], preferred_element_type=f32)
        send[...] = product[pl.ds(pl.multiple_of((1 - core) * half, 16), half), :].astype(bf16)
        keep[k] = product[pl.ds(pl.multiple_of(core * half, 16), half), :]


def gate_up(at, first, up, down, scale, gain, gate_weight, up_weight):
    n = len(up)
    rows, width = up[0].shape
    depth, cols = gate_weight.shape
    half = rows // CORES
    if width % 128 or cols % 256:
        place, core = at[0], at[1]
        normed = jnp.zeros((rows, depth), bf16)
        for t in range(n):
            piece = up[0] if t == 0 else jnp.where(place >= t, up[t], down[n - t])
            piece = (piece.astype(f32) * scale[first : first + rows] * gain[t][None, :]).astype(bf16)
            normed = lax.dynamic_update_slice(normed, piece, (0, lax.rem(place + n - t, n) * width))
        both = jnp.stack(
            [jnp.dot(normed, w, preferred_element_type=f32) for w in (gate_weight, up_weight)]
        ).reshape(2, CORES, half, cols)
        pick = lambda c: lax.dynamic_index_in_dim(both, c, 1, keepdims=False)
        away = pick(1 - core).astype(bf16)
        return away[0], away[1], pick(core)
    tile = 256
    whole = lambda shape: pl.BlockSpec(shape, lambda j, at: (0,) * len(shape))
    weight = pl.BlockSpec((depth, tile), lambda j, at: (0, j))
    result = pl.BlockSpec((2, half, tile), lambda j, at: (0, 0, j))
    away = pl.BlockSpec((half, tile), lambda j, at: (0, j))
    return pl.pallas_call(
        functools.partial(gate_up_kernel, n, first),
        grid_spec=pltpu.PrefetchScalarGridSpec(
            num_scalar_prefetch=1,
            grid=(cols // tile,),
            in_specs=[whole((rows, width))] * (2 * n - 1)
            + [whole(scale.shape), whole((n, width)), weight, weight],
            out_specs=[away, away, result],
            scratch_shapes=[pltpu.VMEM((rows, depth), bf16), pltpu.VMEM((rows, tile), f32)],
        ),
        out_shape=[
            jax.ShapeDtypeStruct((half, cols), bf16),
            jax.ShapeDtypeStruct((half, cols), bf16),
            jax.ShapeDtypeStruct((2, half, cols), f32),
        ],
        compiler_params=pltpu.CompilerParams(vmem_limit_bytes=VMEM),
        cost_estimate=pl.CostEstimate(flops=0, bytes_accessed=0, transcendentals=0),
        name="gate_up",
    )(at, *up, *down[1:], scale, gain, gate_weight, up_weight)


def down_kernel(ring, at, *refs):
    mine, other = refs[:ring], refs[ring : 2 * ring]
    weight, terms, ahead, behind, hidden = refs[2 * ring :]
    core, x = at[1], at[2]
    part = mine[0].shape[0]

    @pl.when(pl.program_id(0) == 0)
    def _():
        for c, pieces in ((core, mine), (1 - core, other)):
            for s in range(ring):
                row = (c * ring + lax.rem(x + (ring - s), ring)) * part
                hidden[pl.ds(pl.multiple_of(row, 16), part), :] = pieces[s][...]

    product = jnp.dot(hidden[...], weight[...], preferred_element_type=f32)
    terms[0] = product

    @pl.when(pl.program_id(0) == pl.num_programs(0) - 1)
    def _():
        ahead[...] = product.astype(bf16)

    @pl.when(pl.program_id(0) == 0)
    def _():
        behind[...] = product.astype(bf16)


def down(at, mine, other, down_weight, n):
    ring = len(mine)
    part, depth = mine[0].shape
    rows = part * ring * CORES
    width = down_weight.shape[1] // n
    if width % 128:
        core, x = at[1], at[2]
        hidden = jnp.zeros((rows, depth), bf16)
        for c, pieces in ((core, mine), (1 - core, other)):
            for s in range(ring):
                row = (c * ring + lax.rem(x + ring - s, ring)) * part
                hidden = lax.dynamic_update_slice(hidden, pieces[s], (row, 0))
        terms = jnp.dot(hidden, down_weight, preferred_element_type=f32)
        terms = terms.reshape(rows, n, width).transpose(1, 0, 2)
        return terms, terms[n - 1].astype(bf16), terms[0].astype(bf16)
    return pl.pallas_call(
        functools.partial(down_kernel, ring),
        grid_spec=pltpu.PrefetchScalarGridSpec(
            num_scalar_prefetch=1,
            grid=(n,),
            in_specs=[pl.BlockSpec((part, depth), lambda j, at: (0, 0))] * (2 * ring)
            + [pl.BlockSpec((depth, width), lambda j, at: (0, j))],
            out_specs=[pl.BlockSpec((1, rows, width), lambda j, at: (j, 0, 0))]
            + [pl.BlockSpec((rows, width), lambda j, at: (0, 0))] * 2,
            scratch_shapes=[pltpu.VMEM((rows, depth), bf16)],
        ),
        out_shape=[jax.ShapeDtypeStruct((n, rows, width), f32)]
        + [jax.ShapeDtypeStruct((rows, width), bf16)] * 2,
        compiler_params=pltpu.CompilerParams(vmem_limit_bytes=VMEM),
        cost_estimate=pl.CostEstimate(flops=0, bytes_accessed=0, transcendentals=0),
        name="down",
    )(at, *mine, *other, down_weight)


class Turn:
    def __init__(self):
        self.held = ()

    def take(self, *values):
        values, _ = lax.optimization_barrier((values, self.held))
        self.held = values
        return values

    def give(self, *values):
        self.held = values


def chunk_blocks(turn, gx, n, at, first, size, tokens, notes, weights, outputs):
    gate_weight, up_weight, down_weight = weights
    place, core, x = at[0], at[1], at[2]
    ring = gx // CORES
    part = size // gx

    (shard,) = turn.take(tokens[first : first + size])
    up, back = [shard], [shard]
    for t in range(1, n):
        up.append(lax.ppermute(up[-1], "gy", [(j, j + 1) for j in range(t - 1, n - 1)]))
        back.append(lax.ppermute(back[-1], "gy", [(j, j - 1) for j in range(1, n - t + 1)]))
        yield
        up[-1], back[-1] = turn.take(up[-1], back[-1])
    *send, keep = gate_up(at, first, up, back, *notes, gate_weight, up_weight)
    turn.give(*send, keep)
    come = [swap_core(value, gx) for value in send]
    yield
    *come, keep = turn.take(*come, keep)
    sums = (keep + jnp.stack(come).astype(f32)).reshape(2, ring, part, keep.shape[2])
    pick = lambda j: lax.dynamic_index_in_dim(sums, j % ring, 1, keepdims=False)
    travelling = None
    for s in range(1, ring):
        share = pick(x + ring - s)
        if travelling is not None:
            share = share + travelling.astype(f32)
        share = share.astype(bf16)
        turn.give(share)
        travelling = rotate(share, "gx", ring, CORES, 1)
        yield
        (travelling,) = turn.take(travelling)
    mine = pick(x) + travelling.astype(f32)
    hidden = (jax.nn.silu(mine[0]) * mine[1]).astype(bf16)
    turn.give(hidden)
    mine, other = [hidden], []
    for s in range(1, ring):
        mine.append(rotate(mine[-1], "gx", ring, CORES, 1))
        other.append(swap_core(mine[-2], gx))
        yield
        (mine[-1],) = turn.take(mine[-1])
    other.append(swap_core(mine[-1], gx))
    yield
    other = turn.take(*other)
    terms, ahead, behind = down(at, mine, other, down_weight, n)
    turn.give(ahead, behind)
    pick = lambda j: lax.dynamic_index_in_dim(terms, jnp.clip(j, 0, n - 1), 0, keepdims=False)
    for o in range(n - 1, 0, -1):
        if o < n - 1:
            ahead = (pick(place + o) + ahead.astype(f32)).astype(bf16)
            behind = (pick(place - o) + behind.astype(f32)).astype(bf16)
            turn.give(ahead, behind)
        ahead = lax.ppermute(ahead, "gy", [(j, j + 1) for j in range(n - o)])
        behind = lax.ppermute(behind, "gy", [(j, j - 1) for j in range(o, n)])
        yield
        ahead, behind = turn.take(ahead, behind)
    total = (pick(place) + ahead.astype(f32) + behind.astype(f32)).astype(bf16)
    turn.give(total)
    outputs[first] = total


def note_blocks(turn, gx, n, tokens, norm_gain, notes):
    ring = gx // CORES
    rows = tokens.shape[0]
    (values,) = turn.take(tokens)
    values = values.astype(f32)
    squares = jnp.sum(values * values, axis=1)
    turn.give(squares)
    other = swap_core(squares, gx)
    yield
    squares, other = turn.take(squares, other)
    squares = squares + other
    turn.give(squares)
    others = [rotate(squares, "gx", ring, CORES, by) for by in range(1, ring)]
    yield
    squares, *others = turn.take(squares, *others)
    note = jnp.concatenate([squares + sum(others), norm_gain.astype(f32)])
    turn.give(note)
    found = [note] + [rotate(note, "gy", n, 1, t) for t in range(1, n)]
    yield
    found = turn.take(*found)
    scale = lax.rsqrt(sum(note[:rows] for note in found) / D + epsilon)[:, None]
    gain = jnp.stack([note[rows:] for note in found])
    turn.give(scale, gain)
    notes.extend((scale, gain))


def local(gx, n, tokens, norm_gain, gate_weight, up_weight, down_weight):
    micro_count, row_count, width = tokens.shape
    rows = micro_count * row_count
    place, index = lax.axis_index("gy"), lax.axis_index("gx")
    at = jnp.stack([place, lax.rem(index, CORES), lax.div(index, CORES)]).astype(jnp.int32)
    tokens = tokens.reshape(rows, width)
    weights = gate_weight, up_weight, down_weight

    turn, notes, outputs = Turn(), [], {}
    chunks, first = [], 0
    for size in CHUNKS if rows == sum(CHUNKS) else (rows,):
        chunks.append(chunk_blocks(turn, gx, n, at, first, size, tokens, notes, weights, outputs))
        first += size
    noting = note_blocks(turn, gx, n, tokens, norm_gain, notes)
    next(chunks[0], None)
    next(noting, None)
    next(noting, None)
    next(chunks[0], None)
    next(noting, None)
    next(chunks[0], None)
    next(noting, None)
    if (n, gx) == (4, 4) and len(chunks) == len(CHUNKS):
        for c in ORDER:
            next(chunks[c], None)
    for chunk in chunks:
        for _ in chunk:
            pass
    return jnp.concatenate([outputs[f] for f in sorted(outputs)]).reshape(micro_count, row_count, width)


def solution(mesh):
    in_specs = (
        P(None, "groups", ("gx", "gy")),
        P(("gx", "gy")),
        P("gx", "gy"),
        P("gx", "gy"),
        P("gy", "gx"),
    )
    out_specs = P(None, "groups", ("gx", "gy"))
    return jax.shard_map(
        functools.partial(local, mesh.shape["gx"], mesh.shape["gy"]),
        mesh=mesh,
        in_specs=in_specs,
        out_specs=out_specs,
        check_vma=False,
    )
```

time: 796 us -> 436 us (0.55)
  waiting for transfers between devices: 642 us -> 115 us
  Pallas kernels: 0 us -> 143 us
  starting transfers between devices: 0.57 us -> 138 us
  matrix products: 90.1 us -> 0 us
  blocking collectives: 35.1 us -> 0 us
  between operations: 13.1 us -> 0.93 us
  local copies, waits for them, and re-layouts: 0.01 us -> 11.5 us
  other arithmetic: 14.7 us -> 26 us
    reduce_scatter x3 -> x0, waiting for transfers between devices: 441 us -> none  [the longest x1 314 us: layer_block(): lax.psum_scatter(terms, 'gy', scatter_dimension=1, tiled=True)]
    all_gather x2 -> x0, waiting for transfers between devices: 201 us -> none  [the longest x1 164 us: layer_block(): shard_piece = lax.all_gather(normed, 'gy', axis=1, tiled=True)]
    pallas_call x0 -> x8, Pallas kernels: none -> 143 us  [the longest x4 91 us: gate_up(): pl.pallas_call(functools.partial(gate_up_kernel, n, first), grid_spec=plt...]
    ppermute x0 -> x77, starting transfers between devices: none -> 138 us  [the longest x12 46.9 us: chunk_blocks(): ahead = lax.ppermute(ahead, 'gy', [(j, j + 1) for j in range(n - o)])]
    ppermute x0 -> x77, waiting for transfers between devices: none -> 115 us  [the longest x12 50.2 us: chunk_blocks(): lax.ppermute(back[-1], 'gy', [(j, j - 1) for j in range(1, n - t + 1)])]
    dot_general x3 -> x0, matrix products: 90.1 us -> none  [the longest x1 30.9 us: layer_block(): up_sum = jnp.dot(shard_piece, up_weight, preferred_element_type=jnp.float32)]
    psum x1 -> x0, blocking collectives: 35.1 us -> none  [layer_block(): squares = lax.psum(jnp.sum(values * values, axis=1), ('gx', 'gy'))]
    convert_element_type x4 -> x17, other arithmetic: 12.4 us -> 16 us  [the longest x8 11.6 us: chunk_blocks(): behind = (pick(place - o) + behind.astype(f32)).astype(bf16)]
  transfers between devices with their start and end apart: 5 -> 77, of which waited for: 5 -> 25; matrix products, arithmetic and copies ran while one was open for 4% -> 6% of each run, Pallas kernels for 0% -> 33%
where the time goes in v1:
time: 436 us; the launch traced here: 434 us
  Pallas kernels  143 us (33%)
  starting transfers between devices  138 us (32%)
  waiting for transfers between devices  115 us (26%)
  other arithmetic  26 us (6%)
  local copies, waits for them, and re-layouts  11.5 us (3%)
    pallas_call x4, Pallas kernels, gate_up(): pl.pallas_call(functools.partial(gate_up_kernel, n, first), grid_spec=plt...  91 us
    pallas_call x4, Pallas kernels, down(): pl.pallas_call(functools.partial(down_kernel, ring), grid_spec=pltpu.Pref...  52 us
    ppermute x12, waiting for transfers between devices, chunk_blocks(): lax.ppermute(back[-1], 'gy', [(j, j - 1) for j in range(1, n - t + 1)])  50.2 us
    ppermute x12, starting transfers between devices, chunk_blocks(): ahead = lax.ppermute(ahead, 'gy', [(j, j + 1) for j in range(n - o)])  46.9 us
    ppermute x12, waiting for transfers between devices, chunk_blocks(): ahead = lax.ppermute(ahead, 'gy', [(j, j + 1) for j in range(n - o)])  41 us
    ppermute x12, starting transfers between devices, chunk_blocks(): lax.ppermute(up[-1], 'gy', [(j, j + 1) for j in range(t - 1, n - 1)])  35.3 us
    ppermute x12, starting transfers between devices, rotate(): return lax.ppermute(value, axis, pairs)  23.8 us
    ppermute x12, starting transfers between devices, chunk_blocks(): lax.ppermute(back[-1], 'gy', [(j, j - 1) for j in range(1, n - t + 1)])  15.6 us
  transfers between devices with their start and end apart: 77, of which 25 were waited for; matrix products, arithmetic and copies ran while one was open for 6% of the time, Pallas kernels for 33%

profile of v1, /device:TPU:0, one launch (start us, length us, event | category | flops | bytes accessed | tf_op | source)
XLA Modules:
  0.0 434.4 jit_solution(11029798425022256357)
XLA Ops:
  3.2 5.6 %collective-permute-start = (bf16[256,1152]{1,0:T(8,128)(2,1)S(1)}, bf16[256,1152]{1,0:T(8,128)(2,1)S(1)}, u32[]{:S(2)}, u32[]{:S(2)}) collective-permute-start(bf16[256,1152]{1,0:T(8,128)(2,1)S(1)} %get-tuple-element.248.refs_0_), channel_id=1, source_target_pairs={{0,1},{1,2},{2,3},{4,5},{5,6},{6,7},{8,9},{9,10},{10,11},{12,13},{... | collective-permute-start | bytes 1769480 | tf_op jit(solution)/shard_map/ppermute | solution.py:184
  10.6 9.6 %collective-permute-done.1.refs_4_ = bf16[256,1152]{1,0:T(8,128)(2,1)S(1)} collective-permute-done((bf16[256,1152]{1,0:T(8,128)(2,1)S(1)}, bf16[256,1152]{1,0:T(8,128)(2,1)S(1)}, u32[]{:S(2)}, u32[]{:S(2)}) %collective-permute-start.1) | collective-permute-done | bytes 589856 | tf_op jit(solution)/shard_map/ppermute | solution.py:185
  28.6 4.7 %collective-permute-start.10 = (f32[2176]{0:T(1024)S(1)}, f32[2176]{0:T(1024)S(1)}, u32[]{:S(2)}, u32[]{:S(2)}) collective-permute-start(f32[2176]{0:T(1024)S(1)} %pad_maximum_fusion.2), channel_id=1, source_target_pairs={{0,3},{1,0},{2,1},{3,2},{4,7},{5,4},{6,5},{7,6},{8,11},{9,8},{10,9... | collective-permute-start | bytes 26120 | tf_op jit(solution)/shard_map/ppermute | solution.py:26
  39.0 4.5 %collective-permute-done.4.refs_5_ = bf16[256,1152]{1,0:T(8,128)(2,1)} collective-permute-done((bf16[256,1152]{1,0:T(8,128)(2,1)S(1)}, bf16[256,1152]{1,0:T(8,128)(2,1)}, u32[]{:S(2)}, u32[]{:S(2)}) %collective-permute-start.4) | collective-permute-done | bytes 589856 | tf_op jit(solution)/shard_map/ppermute | solution.py:185
  46.5 5.4 %collective-permute-start.11 = (bf16[256,1152]{1,0:T(8,128)(2,1)S(1)}, bf16[256,1152]{1,0:T(8,128)(2,1)}, u32[]{:S(2)}, u32[]{:S(2)}) collective-permute-start(bf16[256,1152]{1,0:T(8,128)(2,1)S(1)} %get-tuple-element.130.refs_0_), channel_id=1, source_target_pairs={{0,1},{1,2},{2,3},{4,5},{5,6},{6,7},{8,9},{9,10},{10,11},{12,13},{... | collective-permute-start | bytes 1769480 | tf_op jit(solution)/shard_map/ppermute | solution.py:184
  51.9 7.9 %collective-permute-done.12.refs_4_ = bf16[256,1152]{1,0:T(8,128)(2,1)} collective-permute-done((bf16[256,1152]{1,0:T(8,128)(2,1)S(1)}, bf16[256,1152]{1,0:T(8,128)(2,1)}, u32[]{:S(2)}, u32[]{:S(2)}) %collective-permute-start.12) | collective-permute-done | bytes 589856 | tf_op jit(solution)/shard_map/ppermute | solution.py:185
  68.0 9.6 %collective-permute-start.17 = (bf16[256,1152]{1,0:T(8,128)(2,1)S(1)}, bf16[256,1152]{1,0:T(8,128)(2,1)}, u32[]{:S(2)}, u32[]{:S(2)}) collective-permute-start(bf16[256,1152]{1,0:T(8,128)(2,1)S(1)} %get-tuple-element.133.refs_0_), channel_id=1, source_target_pairs={{0,1},{1,2},{2,3},{4,5},{5,6},{6,7},{8,9},{9,10},{10,11},{12,13},{... | collective-permute-start | bytes 1769480 | tf_op jit(solution)/shard_map/ppermute | solution.py:184
  77.6 5.4 %collective-permute-done.14.refs_5_ = bf16[256,1152]{1,0:T(8,128)(2,1)} collective-permute-done((bf16[256,1152]{1,0:T(8,128)(2,1)}, bf16[256,1152]{1,0:T(8,128)(2,1)}, u32[]{:S(2)}, u32[]{:S(2)}) %collective-permute-start.14) | collective-permute-done | bytes 589856 | tf_op jit(solution)/shard_map/ppermute | solution.py:185
  83.0 12.6 %collective-permute-done.7.refs_6_ = bf16[256,1152]{1,0:T(8,128)(2,1)} collective-permute-done((bf16[256,1152]{1,0:T(8,128)(2,1)}, bf16[256,1152]{1,0:T(8,128)(2,1)}, u32[]{:S(2)}, u32[]{:S(2)}) %collective-permute-start.7) | collective-permute-done | bytes 589856 | tf_op jit(solution)/shard_map/ppermute | solution.py:185
  97.8 22.7 %gate_up.4 = (bf16[128,2304]{1,0:T(8,128)(2,1)}, bf16[128,2304]{1,0:T(8,128)(2,1)}, f32[2,128,2304]{2,1,0:T(8,128)}) custom-call(s32[3]{0:T(128)S(1)} %pad_add_fusion.at, bf16[256,1152]{1,0:T(8,128)(2,1)S(1)} %get-tuple-element.248.refs_0_, bf16[256,1152]{1,0:T(8,128)(2,1)S(1)} %copy-done.9, bf16[256,1152]{1,0:T(8,128)(2,1)} %collective-permute-done.3.refs_2_, ...), custom_call_target="tpu_custom_call" | custom-call | tf_op jit(solution)/shard_map/gate_up/pallas_call | solution.py:82
  131.1 6.0 %collective-permute-start.25 = (bf16[256,1152]{1,0:T(8,128)(2,1)S(1)}, bf16[256,1152]{1,0:T(8,128)(2,1)S(1)}, u32[]{:S(2)}, u32[]{:S(2)}) collective-permute-start(bf16[256,1152]{1,0:T(8,128)(2,1)S(1)} %get-tuple-element.136.refs_0_), channel_id=1, source_target_pairs={{0,1},{1,2},{2,3},{4,5},{5,6},{6,7},{8,9},{9,10},{10,11},{12,13},{... | collective-permute-start | bytes 1769480 | tf_op jit(solution)/shard_map/ppermute | solution.py:184
  140.9 23.1 %gate_up.5 = (bf16[128,2304]{1,0:T(8,128)(2,1)S(1)}, bf16[128,2304]{1,0:T(8,128)(2,1)S(1)}, f32[2,128,2304]{2,1,0:T(8,128)}) custom-call(s32[3]{0:T(128)S(1)} %pad_add_fusion.at, bf16[256,1152]{1,0:T(8,128)(2,1)S(1)} %get-tuple-element.130.refs_0_, bf16[256,1152]{1,0:T(8,128)(2,1)} %collective-permute-done.11.refs_1_, ...), custom_call_target="tpu_custom_call" | custom-call | tf_op jit(solution)/shard_map/gate_up/pallas_call | solution.py:82
  171.2 5.2 %collective-permute-done.22.refs_1_ = bf16[64,2304]{1,0:T(8,128)(2,1)S(1)} collective-permute-done((bf16[64,2304]{1,0:T(8,128)(2,1)S(1)}, bf16[64,2304]{1,0:T(8,128)(2,1)S(1)}, u32[]{:S(2)}, u32[]{:S(2)}) %collective-permute-start.22) | collective-permute-done | bytes 294944 | tf_op jit(solution)/shard_map/ppermute | solution.py:26
  177.8 6.2 %collective-permute-done.30.refs_5_ = bf16[256,1152]{1,0:T(8,128)(2,1)S(1)} collective-permute-done((bf16[256,1152]{1,0:T(8,128)(2,1)S(1)}, bf16[256,1152]{1,0:T(8,128)(2,1)S(1)}, u32[]{:S(2)}, u32[]{:S(2)}) %collective-permute-start.30) | collective-permute-done | bytes 589856 | tf_op jit(solution)/shard_map/ppermute | solution.py:185
  186.9 13.3 %down.4 = (f32[4,256,1152]{2,1,0:T(8,128)}, bf16[256,1152]{1,0:T(8,128)(2,1)}, bf16[256,1152]{1,0:T(8,128)(2,1)}) custom-call(s32[3]{0:T(128)S(1)} %pad_add_fusion.at, bf16[64,2304]{1,0:T(8,128)(2,1)S(1)} %fusion.35.refs_0_, bf16[64,2304]{1,0:T(8,128)(2,1)S(1)} %collective-permute-done.22.refs_1_, bf16[64,2304]{1,0:T(8,128)(2,1)S(1)} %collective-permute-done.27.refs_2_, ...), custom_call_target="tpu_custom_call" | custom-call | tf_op jit(solution)/shard_map/down/pallas_call | solution.py:143
  200.2 5.5 %collective-permute-start.31 = (bf16[256,1152]{1,0:T(8,128)(2,1)}, bf16[256,1152]{1,0:T(8,128)(2,1)}, u32[]{:S(2)}, u32[]{:S(2)}) collective-permute-start(bf16[256,1152]{1,0:T(8,128)(2,1)} %get-tuple-element.164), channel_id=1, source_target_pairs={{0,1},{4,5},{8,9},{12,13},{16,17},{20,21},{24,25},{28,29}} | collective-permute-start | bytes 1769480 | tf_op jit(solution)/shard_map/ppermute | solution.py:225
  208.5 22.9 %gate_up.6 = (bf16[128,2304]{1,0:T(8,128)(2,1)}, bf16[128,2304]{1,0:T(8,128)(2,1)}, f32[2,128,2304]{2,1,0:T(8,128)}) custom-call(s32[3]{0:T(128)S(1)} %pad_add_fusion.at, bf16[256,1152]{1,0:T(8,128)(2,1)S(1)} %get-tuple-element.133.refs_0_, bf16[256,1152]{1,0:T(8,128)(2,1)} %collective-permute-done.17.refs_1_, ...), custom_call_target="tpu_custom_call" | custom-call | tf_op jit(solution)/shard_map/gate_up/pallas_call | solution.py:82
  247.8 12.9 %down.5 = (f32[4,256,1152]{2,1,0:T(8,128)}, bf16[256,1152]{1,0:T(8,128)(2,1)S(1)}, bf16[256,1152]{1,0:T(8,128)(2,1)S(1)}) custom-call(s32[3]{0:T(128)S(1)} %pad_add_fusion.at, bf16[64,2304]{1,0:T(8,128)(2,1)S(1)} %fusion.33.refs_0_, bf16[64,2304]{1,0:T(8,128)(2,1)S(1)} %collective-permute-done.42.refs_1_, ...), custom_call_target="tpu_custom_call" | custom-call | tf_op jit(solution)/shard_map/down/pallas_call | solution.py:143
  262.7 22.3 %gate_up.7 = (bf16[128,2304]{1,0:T(8,128)(2,1)S(1)}, bf16[128,2304]{1,0:T(8,128)(2,1)S(1)}, f32[2,128,2304]{2,1,0:T(8,128)}) custom-call(s32[3]{0:T(128)S(1)} %pad_add_fusion.at, bf16[256,1152]{1,0:T(8,128)(2,1)S(1)} %get-tuple-element.136.refs_0_, bf16[256,1152]{1,0:T(8,128)(2,1)S(1)} %copy-done.1, bf16[256,1152]{1,0:T(8,128)(2,1)S(1)} %copy-done.3, ...), custom_call_target="tpu_custom_call" | custom-call | tf_op jit(solution)/shard_map/gate_up/pallas_call | solution.py:82
  298.7 4.7 %collective-permute-start.59 = (bf16[256,1152]{1,0:T(8,128)(2,1)S(1)}, bf16[256,1152]{1,0:T(8,128)(2,1)S(1)}, u32[]{:S(2)}, u32[]{:S(2)}) collective-permute-start(bf16[256,1152]{1,0:T(8,128)(2,1)S(1)} %get-tuple-element.242), channel_id=1, source_target_pairs={{0,1},{1,2},{4,5},{5,6},{8,9},{9,10},{12,13},{13,14},{16,17},{17,1... | collective-permute-start | bytes 1769480 | tf_op jit(solution)/shard_map/ppermute | solution.py:225
  306.5 13.0 %down.6 = (f32[4,256,1152]{2,1,0:T(8,128)}, bf16[256,1152]{1,0:T(8,128)(2,1)S(1)}, bf16[256,1152]{1,0:T(8,128)(2,1)S(1)}) custom-call(s32[3]{0:T(128)S(1)} %pad_add_fusion.at, bf16[64,2304]{1,0:T(8,128)(2,1)S(1)} %fusion.31.refs_0_, bf16[64,2304]{1,0:T(8,128)(2,1)S(1)} %collective-permute-done.48.refs_1_, ...), custom_call_target="tpu_custom_call" | custom-call | tf_op jit(solution)/shard_map/down/pallas_call | solution.py:143
  325.8 6.0 %collective-permute-start.67 = (bf16[256,1152]{1,0:T(8,128)(2,1)}, bf16[256,1152]{1,0:T(8,128)(2,1)}, u32[]{:S(2)}, u32[]{:S(2)}) collective-permute-start(bf16[256,1152]{1,0:T(8,128)(2,1)} %get-tuple-element.238), channel_id=1, source_target_pairs={{0,1},{1,2},{2,3},{4,5},{5,6},{6,7},{8,9},{9,10},{10,11},{12,13},{... | collective-permute-start | bytes 1769480 | tf_op jit(solution)/shard_map/ppermute | solution.py:225
  339.1 12.9 %down.7 = (f32[4,256,1152]{2,1,0:T(8,128)}, bf16[256,1152]{1,0:T(8,128)(2,1)S(1)}, bf16[256,1152]{1,0:T(8,128)(2,1)S(1)}) custom-call(s32[3]{0:T(128)S(1)} %pad_add_fusion.at, bf16[64,2304]{1,0:T(8,128)(2,1)S(1)} %fusion.29.refs_0_, bf16[64,2304]{1,0:T(8,128)(2,1)S(1)} %collective-permute-done.58.refs_1_, ...), custom_call_target="tpu_custom_call" | custom-call | tf_op jit(solution)/shard_map/down/pallas_call | solution.py:143
  352.0 4.6 %collective-permute-start.63 = (bf16[256,1152]{1,0:T(8,128)(2,1)S(1)}, bf16[256,1152]{1,0:T(8,128)(2,1)S(1)}, u32[]{:S(2)}, u32[]{:S(2)}) collective-permute-start(bf16[256,1152]{1,0:T(8,128)(2,1)S(1)} %get-tuple-element.210), channel_id=1, source_target_pairs={{0,1},{4,5},{8,9},{12,13},{16,17},{20,21},{24,25},{28,29}} | collective-permute-start | bytes 1769480 | tf_op jit(solution)/shard_map/ppermute | solution.py:225
  364.9 5.4 %collective-permute-done.63 = bf16[256,1152]{1,0:T(8,128)(2,1)S(1)} collective-permute-done((bf16[256,1152]{1,0:T(8,128)(2,1)S(1)}, bf16[256,1152]{1,0:T(8,128)(2,1)S(1)}, u32[]{:S(2)}, u32[]{:S(2)}) %collective-permute-start.63) | collective-permute-done | bytes 589856 | tf_op jit(solution)/shard_map/ppermute | solution.py:225
  378.2 4.7 %collective-permute-done.53 = bf16[256,1152]{1,0:T(8,128)(2,1)S(1)} collective-permute-done((bf16[256,1152]{1,0:T(8,128)(2,1)S(1)}, bf16[256,1152]{1,0:T(8,128)(2,1)S(1)}, u32[]{:S(2)}, u32[]{:S(2)}) %collective-permute-start.53) | collective-permute-done | bytes 589856 | tf_op jit(solution)/shard_map/ppermute | solution.py:225
  384.4 11.1 %collective-permute-done.71 = bf16[256,1152]{1,0:T(8,128)(2,1)S(1)} collective-permute-done((bf16[256,1152]{1,0:T(8,128)(2,1)S(1)}, bf16[256,1152]{1,0:T(8,128)(2,1)S(1)}, u32[]{:S(2)}, u32[]{:S(2)}) %collective-permute-start.71) | collective-permute-done | bytes 589856 | tf_op jit(solution)/shard_map/ppermute | solution.py:225
  397.1 5.1 %collective-permute-start.75 = (bf16[256,1152]{1,0:T(8,128)(2,1)S(1)}, bf16[256,1152]{1,0:T(8,128)(2,1)S(1)}, u32[]{:S(2)}, u32[]{:S(2)}) collective-permute-start(bf16[256,1152]{1,0:T(8,128)(2,1)S(1)} %get-tuple-element.232), channel_id=1, source_target_pairs={{0,1},{1,2},{2,3},{4,5},{5,6},{6,7},{8,9},{9,10},{10,11},{12,13},{... | collective-permute-start | bytes 1769480 | tf_op jit(solution)/shard_map/ppermute | solution.py:225
  402.2 6.0 %collective-permute-done.69 = bf16[256,1152]{1,0:T(8,128)(2,1)S(1)} collective-permute-done((bf16[256,1152]{1,0:T(8,128)(2,1)S(1)}, bf16[256,1152]{1,0:T(8,128)(2,1)S(1)}, u32[]{:S(2)}, u32[]{:S(2)}) %collective-permute-start.69) | collective-permute-done | bytes 589856 | tf_op jit(solution)/shard_map/ppermute | solution.py:225
  409.8 5.1 %collective-permute-start.73 = (bf16[256,1152]{1,0:T(8,128)(2,1)S(1)}, bf16[256,1152]{1,0:T(8,128)(2,1)S(1)}, u32[]{:S(2)}, u32[]{:S(2)}) collective-permute-start(bf16[256,1152]{1,0:T(8,128)(2,1)S(1)} %get-tuple-element.230), channel_id=1, source_target_pairs={{0,1},{1,2},{2,3},{4,5},{5,6},{6,7},{8,9},{9,10},{10,11},{12,13},{... | collective-permute-start | bytes 1769480 | tf_op jit(solution)/shard_map/ppermute | solution.py:225
  414.9 6.0 %collective-permute-done.75 = bf16[256,1152]{1,0:T(8,128)(2,1)S(1)} collective-permute-done((bf16[256,1152]{1,0:T(8,128)(2,1)S(1)}, bf16[256,1152]{1,0:T(8,128)(2,1)S(1)}, u32[]{:S(2)}, u32[]{:S(2)}) %collective-permute-start.75) | collective-permute-done | bytes 589856 | tf_op jit(solution)/shard_map/ppermute | solution.py:225
  424.7 7.8 %collective-permute-done.73 = bf16[256,1152]{1,0:T(8,128)(2,1)S(1)} collective-permute-done((bf16[256,1152]{1,0:T(8,128)(2,1)S(1)}, bf16[256,1152]{1,0:T(8,128)(2,1)S(1)}, u32[]{:S(2)}, u32[]{:S(2)}) %collective-permute-start.73) | collective-permute-done | bytes 589856 | tf_op jit(solution)/shard_map/ppermute | solution.py:225
  (229 shorter events, 136.0 us)
Async XLA Ops:
  65.1 30.6 %collective-permute-start.7 = (bf16[256,1152]{1,0:T(8,128)(2,1)}, bf16[256,1152]{1,0:T(8,128)(2,1)}, u32[]{:S(2)}, u32[]{:S(2)}) collective-permute-start(bf16[256,1152]{1,0:T(8,128)(2,1)} %collective-permute-done.4.refs_5_), channel_id=1, source_target_pairs={{1,0},{5,4},{9,8},{13,12},{17,16},{21,20},{25,24},{29,28}} | collective-permute-start | bytes 1769480 | tf_op jit(solution)/shard_map/ppermute | solution.py:185
  66.7 55.8 %collective-permute-start.18 = (bf16[256,1152]{1,0:T(8,128)(2,1)S(1)}, bf16[256,1152]{1,0:T(8,128)(2,1)S(1)}, u32[]{:S(2)}, u32[]{:S(2)}) collective-permute-start(bf16[256,1152]{1,0:T(8,128)(2,1)S(1)} %get-tuple-element.133.refs_0_), channel_id=1, source_target_pairs={{1,0},{2,1},{3,2},{5,4},{6,5},{7,6},{9,8},{10,9},{11,10},{13,12},{... | collective-permute-start | bytes 1769480 | tf_op jit(solution)/shard_map/ppermute | solution.py:185
  68.0 55.8 %collective-permute-start.17 = (bf16[256,1152]{1,0:T(8,128)(2,1)S(1)}, bf16[256,1152]{1,0:T(8,128)(2,1)}, u32[]{:S(2)}, u32[]{:S(2)}) collective-permute-start(bf16[256,1152]{1,0:T(8,128)(2,1)S(1)} %get-tuple-element.133.refs_0_), channel_id=1, source_target_pairs={{0,1},{1,2},{2,3},{4,5},{5,6},{6,7},{8,9},{9,10},{10,11},{12,13},{... | collective-permute-start | bytes 1769480 | tf_op jit(solution)/shard_map/ppermute | solution.py:184
  128.1 35.8 %collective-permute-start.19 = (bf16[2,64,2304]{2,1,0:T(8,128)(2,1)}, bf16[2,64,2304]{2,1,0:T(8,128)(2,1)}, u32[]{:S(2)}, u32[]{:S(2)}) collective-permute-start(bf16[2,64,2304]{2,1,0:T(8,128)(2,1)} %fusion.24), channel_id=1, source_target_pairs={{0,8},{4,12},{8,0},{12,4},{1,9},{5,13},{9,1},{13,5},{2,10},{6,14},... | collective-permute-start | bytes 1769480 | tf_op jit(solution)/shard_map/ppermute | solution.py:26
  129.6 36.3 %collective-permute-start.26 = (bf16[256,1152]{1,0:T(8,128)(2,1)S(1)}, bf16[256,1152]{1,0:T(8,128)(2,1)S(1)}, u32[]{:S(2)}, u32[]{:S(2)}) collective-permute-start(bf16[256,1152]{1,0:T(8,128)(2,1)S(1)} %get-tuple-element.136.refs_0_), channel_id=1, source_target_pairs={{1,0},{2,1},{3,2},{5,4},{6,5},{7,6},{9,8},{10,9},{11,10},{13,12},{... | collective-permute-start | bytes 1769480 | tf_op jit(solution)/shard_map/ppermute | solution.py:185
  131.1 36.2 %collective-permute-start.25 = (bf16[256,1152]{1,0:T(8,128)(2,1)S(1)}, bf16[256,1152]{1,0:T(8,128)(2,1)S(1)}, u32[]{:S(2)}, u32[]{:S(2)}) collective-permute-start(bf16[256,1152]{1,0:T(8,128)(2,1)S(1)} %get-tuple-element.136.refs_0_), channel_id=1, source_target_pairs={{0,1},{1,2},{2,3},{4,5},{5,6},{6,7},{8,9},{9,10},{10,11},{12,13},{... | collective-permute-start | bytes 1769480 | tf_op jit(solution)/shard_map/ppermute | solution.py:184
  137.1 40.7 %collective-permute-start.29 = (bf16[256,1152]{1,0:T(8,128)(2,1)}, bf16[256,1152]{1,0:T(8,128)(2,1)S(1)}, u32[]{:S(2)}, u32[]{:S(2)}) collective-permute-start(bf16[256,1152]{1,0:T(8,128)(2,1)} %collective-permute-done.17.refs_1_), channel_id=1, source_target_pairs={{1,2},{2,3},{5,6},{6,7},{9,10},{10,11},{13,14},{14,15},{17,18},{18... | collective-permute-start | bytes 1769480 | tf_op jit(solution)/shard_map/ppermute | solution.py:184
  168.9 31.3 %collective-permute-start.36 = (bf16[256,1152]{1,0:T(8,128)(2,1)S(1)}, bf16[256,1152]{1,0:T(8,128)(2,1)S(1)}, u32[]{:S(2)}, u32[]{:S(2)}) collective-permute-start(bf16[256,1152]{1,0:T(8,128)(2,1)S(1)} %collective-permute-done.25.refs_1_), channel_id=1, source_target_pairs={{1,2},{2,3},{5,6},{6,7},{9,10},{10,11},{13,14},{14,15},{17,18},{18... | collective-permute-start | bytes 1769480 | tf_op jit(solution)/shard_map/ppermute | solution.py:184
  169.6 36.1 %collective-permute-start.37 = (bf16[256,1152]{1,0:T(8,128)(2,1)S(1)}, bf16[256,1152]{1,0:T(8,128)(2,1)S(1)}, u32[]{:S(2)}, u32[]{:S(2)}) collective-permute-start(bf16[256,1152]{1,0:T(8,128)(2,1)S(1)} %collective-permute-done.26.refs_4_), channel_id=1, source_target_pairs={{1,0},{2,1},{5,4},{6,5},{9,8},{10,9},{13,12},{14,13},{17,16},{18,1... | collective-permute-start | bytes 1769480 | tf_op jit(solution)/shard_map/ppermute | solution.py:185
  176.3 30.8 %collective-permute-start.35 = (bf16[2,64,2304]{2,1,0:T(8,128)(2,1)S(1)}, bf16[2,64,2304]{2,1,0:T(8,128)(2,1)S(1)}, u32[]{:S(2)}, u32[]{:S(2)}) collective-permute-start(bf16[2,64,2304]{2,1,0:T(8,128)(2,1)S(1)} %fusion.25), channel_id=1, source_target_pairs={{0,8},{4,12},{8,0},{12,4},{1,9},{5,13},{9,1},{13,5},{2,10},{6,14},... | collective-permute-start | bytes 1769480 | tf_op jit(solution)/shard_map/ppermute | solution.py:26
  184.1 23.4 %collective-permute-start.33 = (bf16[256,1152]{1,0:T(8,128)(2,1)S(1)}, bf16[256,1152]{1,0:T(8,128)(2,1)S(1)}, u32[]{:S(2)}, u32[]{:S(2)}) collective-permute-start(bf16[256,1152]{1,0:T(8,128)(2,1)S(1)} %collective-permute-done.29.refs_2_), channel_id=1, source_target_pairs={{2,3},{6,7},{10,11},{14,15},{18,19},{22,23},{26,27},{30,31}} | collective-permute-start | bytes 1769480 | tf_op jit(solution)/shard_map/ppermute | solution.py:184
  200.2 33.2 %collective-permute-start.31 = (bf16[256,1152]{1,0:T(8,128)(2,1)}, bf16[256,1152]{1,0:T(8,128)(2,1)}, u32[]{:S(2)}, u32[]{:S(2)}) collective-permute-start(bf16[256,1152]{1,0:T(8,128)(2,1)} %get-tuple-element.164), channel_id=1, source_target_pairs={{0,1},{4,5},{8,9},{12,13},{16,17},{20,21},{24,25},{28,29}} | collective-permute-start | bytes 1769480 | tf_op jit(solution)/shard_map/ppermute | solution.py:225
  205.7 28.4 %collective-permute-start.32 = (bf16[256,1152]{1,0:T(8,128)(2,1)}, bf16[256,1152]{1,0:T(8,128)(2,1)}, u32[]{:S(2)}, u32[]{:S(2)}) collective-permute-start(bf16[256,1152]{1,0:T(8,128)(2,1)} %get-tuple-element.165), channel_id=1, source_target_pairs={{3,2},{7,6},{11,10},{15,14},{19,18},{23,22},{27,26},{31,30}} | collective-permute-start | bytes 1769480 | tf_op jit(solution)/shard_map/ppermute | solution.py:226
  233.4 28.6 %collective-permute-start.44 = (bf16[256,1152]{1,0:T(8,128)(2,1)}, bf16[256,1152]{1,0:T(8,128)(2,1)S(1)}, u32[]{:S(2)}, u32[]{:S(2)}) collective-permute-start(bf16[256,1152]{1,0:T(8,128)(2,1)} %copy-done.2), channel_id=1, source_target_pairs={{2,3},{6,7},{10,11},{14,15},{18,19},{22,23},{26,27},{30,31}} | collective-permute-start | bytes 1769480 | tf_op jit(solution)/shard_map/ppermute | solution.py:184
  234.1 28.6 %collective-permute-start.45 = (bf16[256,1152]{1,0:T(8,128)(2,1)}, bf16[256,1152]{1,0:T(8,128)(2,1)S(1)}, u32[]{:S(2)}, u32[]{:S(2)}) collective-permute-start(bf16[256,1152]{1,0:T(8,128)(2,1)} %copy-done.4), channel_id=1, source_target_pairs={{1,0},{5,4},{9,8},{13,12},{17,16},{21,20},{25,24},{29,28}} | collective-permute-start | bytes 1769480 | tf_op jit(solution)/shard_map/ppermute | solution.py:185
  243.2 41.9 %collective-permute-start.43 = (bf16[2,64,2304]{2,1,0:T(8,128)(2,1)}, bf16[2,64,2304]{2,1,0:T(8,128)(2,1)}, u32[]{:S(2)}, u32[]{:S(2)}) collective-permute-start(bf16[2,64,2304]{2,1,0:T(8,128)(2,1)} %fusion.26), channel_id=1, source_target_pairs={{0,8},{4,12},{8,0},{12,4},{1,9},{5,13},{9,1},{13,5},{2,10},{6,14},... | collective-permute-start | bytes 1769480 | tf_op jit(solution)/shard_map/ppermute | solution.py:26
  246.3 52.4 %collective-permute-start.39 = (bf16[256,1152]{1,0:T(8,128)(2,1)}, bf16[256,1152]{1,0:T(8,128)(2,1)}, u32[]{:S(2)}, u32[]{:S(2)}) collective-permute-start(bf16[256,1152]{1,0:T(8,128)(2,1)} %get-tuple-element.243), channel_id=1, source_target_pairs={{2,1},{3,2},{6,5},{7,6},{10,9},{11,10},{14,13},{15,14},{18,17},{19... | collective-permute-start | bytes 1769480 | tf_op jit(solution)/shard_map/ppermute | solution.py:226
  260.6 26.3 %collective-permute-start.51 = (bf16[256,1152]{1,0:T(8,128)(2,1)S(1)}, bf16[256,1152]{1,0:T(8,128)(2,1)S(1)}, u32[]{:S(2)}, u32[]{:S(2)}) collective-permute-start(bf16[256,1152]{1,0:T(8,128)(2,1)S(1)} %get-tuple-element.182), channel_id=1, source_target_pairs={{0,1},{4,5},{8,9},{12,13},{16,17},{20,21},{24,25},{28,29}} | collective-permute-start | bytes 1769480 | tf_op jit(solution)/shard_map/ppermute | solution.py:225
  262.0 26.3 %collective-permute-start.52 = (bf16[256,1152]{1,0:T(8,128)(2,1)S(1)}, bf16[256,1152]{1,0:T(8,128)(2,1)S(1)}, u32[]{:S(2)}, u32[]{:S(2)}) collective-permute-start(bf16[256,1152]{1,0:T(8,128)(2,1)S(1)} %get-tuple-element.183), channel_id=1, source_target_pairs={{3,2},{7,6},{11,10},{15,14},{19,18},{23,22},{27,26},{31,30}} | collective-permute-start | bytes 1769480 | tf_op jit(solution)/shard_map/ppermute | solution.py:226
  294.1 25.4 %collective-permute-start.55 = (bf16[2,64,2304]{2,1,0:T(8,128)(2,1)}, bf16[2,64,2304]{2,1,0:T(8,128)(2,1)}, u32[]{:S(2)}, u32[]{:S(2)}) collective-permute-start(bf16[2,64,2304]{2,1,0:T(8,128)(2,1)} %fusion.27), channel_id=1, source_target_pairs={{0,8},{4,12},{8,0},{12,4},{1,9},{5,13},{9,1},{13,5},{2,10},{6,14},... | collective-permute-start | bytes 1769480 | tf_op jit(solution)/shard_map/ppermute | solution.py:26
  298.0 25.1 %collective-permute-start.60 = (bf16[256,1152]{1,0:T(8,128)(2,1)}, bf16[256,1152]{1,0:T(8,128)(2,1)S(1)}, u32[]{:S(2)}, u32[]{:S(2)}) collective-permute-start(bf16[256,1152]{1,0:T(8,128)(2,1)} %get-tuple-element.241), channel_id=1, source_target_pairs={{2,1},{3,2},{6,5},{7,6},{10,9},{11,10},{14,13},{15,14},{18,17},{19... | collective-permute-start | bytes 1769480 | tf_op jit(solution)/shard_map/ppermute | solution.py:226
  298.7 24.4 %collective-permute-start.59 = (bf16[256,1152]{1,0:T(8,128)(2,1)S(1)}, bf16[256,1152]{1,0:T(8,128)(2,1)S(1)}, u32[]{:S(2)}, u32[]{:S(2)}) collective-permute-start(bf16[256,1152]{1,0:T(8,128)(2,1)S(1)} %get-tuple-element.242), channel_id=1, source_target_pairs={{0,1},{1,2},{4,5},{5,6},{8,9},{9,10},{12,13},{13,14},{16,17},{17,1... | collective-permute-start | bytes 1769480 | tf_op jit(solution)/shard_map/ppermute | solution.py:225
  324.3 27.7 %collective-permute-start.68 = (bf16[256,1152]{1,0:T(8,128)(2,1)}, bf16[256,1152]{1,0:T(8,128)(2,1)}, u32[]{:S(2)}, u32[]{:S(2)}) collective-permute-start(bf16[256,1152]{1,0:T(8,128)(2,1)} %get-tuple-element.237), channel_id=1, source_target_pairs={{1,0},{2,1},{3,2},{5,4},{6,5},{7,6},{9,8},{10,9},{11,10},{13,12},{... | collective-permute-start | bytes 1769480 | tf_op jit(solution)/shard_map/ppermute | solution.py:226
  325.8 30.7 %collective-permute-start.67 = (bf16[256,1152]{1,0:T(8,128)(2,1)}, bf16[256,1152]{1,0:T(8,128)(2,1)}, u32[]{:S(2)}, u32[]{:S(2)}) collective-permute-start(bf16[256,1152]{1,0:T(8,128)(2,1)} %get-tuple-element.238), channel_id=1, source_target_pairs={{0,1},{1,2},{2,3},{4,5},{5,6},{6,7},{8,9},{9,10},{10,11},{12,13},{... | collective-permute-start | bytes 1769480 | tf_op jit(solution)/shard_map/ppermute | solution.py:225
  332.3 26.8 %collective-permute-start.65 = (bf16[256,1152]{1,0:T(8,128)(2,1)S(1)}, bf16[256,1152]{1,0:T(8,128)(2,1)}, u32[]{:S(2)}, u32[]{:S(2)}) collective-permute-start(bf16[256,1152]{1,0:T(8,128)(2,1)S(1)} %get-tuple-element.201), channel_id=1, source_target_pairs={{0,1},{4,5},{8,9},{12,13},{16,17},{20,21},{24,25},{28,29}} | collective-permute-start | bytes 1769480 | tf_op jit(solution)/shard_map/ppermute | solution.py:225
  336.3 25.4 %collective-permute-start.66 = (bf16[256,1152]{1,0:T(8,128)(2,1)S(1)}, bf16[256,1152]{1,0:T(8,128)(2,1)}, u32[]{:S(2)}, u32[]{:S(2)}) collective-permute-start(bf16[256,1152]{1,0:T(8,128)(2,1)S(1)} %get-tuple-element.202), channel_id=1, source_target_pairs={{3,2},{7,6},{11,10},{15,14},{19,18},{23,22},{27,26},{31,30}} | collective-permute-start | bytes 1769480 | tf_op jit(solution)/shard_map/ppermute | solution.py:226
  337.8 37.9 %collective-permute-start.54 = (bf16[256,1152]{1,0:T(8,128)(2,1)}, bf16[256,1152]{1,0:T(8,128)(2,1)S(1)}, u32[]{:S(2)}, u32[]{:S(2)}) collective-permute-start(bf16[256,1152]{1,0:T(8,128)(2,1)} %get-tuple-element.239), channel_id=1, source_target_pairs={{1,0},{2,1},{3,2},{5,4},{6,5},{7,6},{9,8},{10,9},{11,10},{13,12},{... | collective-permute-start | bytes 1769480 | tf_op jit(solution)/shard_map/ppermute | solution.py:226
  359.1 23.8 %collective-permute-start.53 = (bf16[256,1152]{1,0:T(8,128)(2,1)S(1)}, bf16[256,1152]{1,0:T(8,128)(2,1)S(1)}, u32[]{:S(2)}, u32[]{:S(2)}) collective-permute-start(bf16[256,1152]{1,0:T(8,128)(2,1)S(1)} %get-tuple-element.240), channel_id=1, source_target_pairs={{0,1},{1,2},{2,3},{4,5},{5,6},{6,7},{8,9},{9,10},{10,11},{12,13},{... | collective-permute-start | bytes 1769480 | tf_op jit(solution)/shard_map/ppermute | solution.py:225
  370.3 25.3 %collective-permute-start.71 = (bf16[256,1152]{1,0:T(8,128)(2,1)S(1)}, bf16[256,1152]{1,0:T(8,128)(2,1)S(1)}, u32[]{:S(2)}, u32[]{:S(2)}) collective-permute-start(bf16[256,1152]{1,0:T(8,128)(2,1)S(1)} %get-tuple-element.236), channel_id=1, source_target_pairs={{0,1},{1,2},{4,5},{5,6},{8,9},{9,10},{12,13},{13,14},{16,17},{17,1... | collective-permute-start | bytes 1769480 | tf_op jit(solution)/shard_map/ppermute | solution.py:225
  375.0 27.2 %collective-permute-start.70 = (bf16[256,1152]{1,0:T(8,128)(2,1)S(1)}, bf16[256,1152]{1,0:T(8,128)(2,1)S(1)}, u32[]{:S(2)}, u32[]{:S(2)}) collective-permute-start(bf16[256,1152]{1,0:T(8,128)(2,1)S(1)} %get-tuple-element.233), channel_id=1, source_target_pairs={{2,1},{3,2},{6,5},{7,6},{10,9},{11,10},{14,13},{15,14},{18,17},{19... | collective-permute-start | bytes 1769480 | tf_op jit(solution)/shard_map/ppermute | solution.py:226
  375.7 32.5 %collective-permute-start.69 = (bf16[256,1152]{1,0:T(8,128)(2,1)S(1)}, bf16[256,1152]{1,0:T(8,128)(2,1)S(1)}, u32[]{:S(2)}, u32[]{:S(2)}) collective-permute-start(bf16[256,1152]{1,0:T(8,128)(2,1)S(1)} %get-tuple-element.234), channel_id=1, source_target_pairs={{0,1},{1,2},{4,5},{5,6},{8,9},{9,10},{12,13},{13,14},{16,17},{17,1... | collective-permute-start | bytes 1769480 | tf_op jit(solution)/shard_map/ppermute | solution.py:225
  397.1 23.7 %collective-permute-start.75 = (bf16[256,1152]{1,0:T(8,128)(2,1)S(1)}, bf16[256,1152]{1,0:T(8,128)(2,1)S(1)}, u32[]{:S(2)}, u32[]{:S(2)}) collective-permute-start(bf16[256,1152]{1,0:T(8,128)(2,1)S(1)} %get-tuple-element.232), channel_id=1, source_target_pairs={{0,1},{1,2},{2,3},{4,5},{5,6},{6,7},{8,9},{9,10},{10,11},{12,13},{... | collective-permute-start | bytes 1769480 | tf_op jit(solution)/shard_map/ppermute | solution.py:225
  (70 other events, 869.2 us)

commit v2 on v0

v2 whole, which is shorter than its diff:
```python
import functools

import jax
import jax.numpy as jnp
from jax import lax
from jax.experimental import pallas as pl
from jax.experimental.pallas import tpu as pltpu
from jax.sharding import PartitionSpec as P

D = 18432
CHUNKS = (384, 384, 256)
ORDER = (1, 0, 1, 0, 0, 2, 1, 1, 0, 2, 1, 0, 2, 1, 2, 0, 2, 1, 2, 0, 1, 2, 0, 2, 1, 2, 1, 2, 1, 2)
VMEM = 48 * 1024 * 1024
bf16, f32 = jnp.bfloat16, jnp.float32
PAIRS = [(0, 1), (1, 0), (2, 3), (3, 2)]
MIDDLE = [(1, 2), (2, 1)]
INWARD = [(0, 1), (3, 2)]
OUTWARD = [(1, 0), (2, 3)]
SWAP_CORE = [(0, 1), (1, 0), (2, 3), (3, 2)]
SWAP_X = [(0, 2), (1, 3), (2, 0), (3, 1)]
PLACE, CORE, X, SIDE, TWIN = range(5)


epsilon = 1e-05


def kernel_call(body, grid, ins, outs, shapes, scratch, name):
    return pl.pallas_call(
        body,
        grid_spec=pltpu.PrefetchScalarGridSpec(
            num_scalar_prefetch=1, grid=(grid,), in_specs=ins, out_specs=outs, scratch_shapes=scratch
        ),
        out_shape=[jax.ShapeDtypeStruct(*shape) for shape in shapes],
        compiler_params=pltpu.CompilerParams(vmem_limit_bytes=VMEM),
        cost_estimate=pl.CostEstimate(flops=0, bytes_accessed=0, transcendentals=0),
        name=name,
    )


def whole(*shape):
    return pl.BlockSpec(shape, lambda j, at: (0,) * len(shape))


def normalize(at, rows, shard, source, scale, gain, normed, column):
    behind = lax.rem(at[PLACE] + 4 - shard, 4)
    values = source[...].astype(f32) * scale[rows, :] * gain[pl.ds(behind, 1), :]
    normed[:, pl.ds(column, source.shape[1])] = values.astype(bf16)


def early_kernel(rows, at, own, pair, inner, outer, scale, gain, *refs):
    weights, sums, normed = refs[:6], refs[6], refs[7]
    width = own.shape[1]
    place, side = at[PLACE], at[SIDE]

    @pl.when(pl.program_id(0) == 0)
    def _():
        def fill(shard, source):
            column = pl.multiple_of((shard - side) * width, 128)
            normalize(at, rows, shard, source, scale, gain, normed, column)

        fill(place, own)
        fill(at[TWIN], pair)
        middle = (place == 1) | (place == 2)
        pl.when(middle)(lambda: fill(2 - side, inner))
        pl.when(jnp.logical_not(middle))(lambda: fill(2 - side, outer))

    for k in range(2):
        total = None
        for m in range(3):
            term = jnp.dot(
                normed[:, m * width : (m + 1) * width], weights[3 * k + m][...], preferred_element_type=f32
            )
            total = term if total is None else total + term
        sums[k] = total


def early(at, rows, own, pair, inner, outer, scale, gain, gate_weight, up_weight):
    size, width = own.shape
    cols = gate_weight.shape[1]
    tile = 256
    blocks = [pl.BlockSpec((width, tile), lambda j, at, m=m: (at[SIDE] + m, j)) for m in range(3)]
    return kernel_call(
        functools.partial(early_kernel, rows),
        cols // tile,
        [whole(size, width)] * 4 + [whole(*scale.shape), whole(*gain.shape)] + blocks * 2,
        [pl.BlockSpec((2, size, tile), lambda j, at: (0, 0, j))],
        [((2, size, cols), f32)],
        [pltpu.VMEM((size, 3 * width), bf16)],
        "early",
    )(at, own, pair, inner, outer, scale, gain, *[gate_weight] * 3, *[up_weight] * 3)[0]


def late_kernel(rows, at, inner, outer, scale, gain, gate_w, up_w, sums, send_gate, send_up, keep, normed, product):
    place, core, far = at[PLACE], at[CORE], 3 - 3 * at[SIDE]
    half = keep.shape[1]

    @pl.when(pl.program_id(0) == 0)
    def _():
        middle = (place == 1) | (place == 2)
        fill = lambda source: normalize(at, rows, far, source, scale, gain, normed, 0)
        pl.when(middle)(lambda: fill(inner))
        pl.when(jnp.logical_not(middle))(lambda: fill(outer))

    for k, (weight, send) in enumerate(((gate_w, send_gate), (up_w, send_up))):
        product[...] = sums[k] + jnp.dot(normed[...], weight[...], preferred_element_type=f32)
        send[...] = product[pl.ds(pl.multiple_of((1 - core) * half, 16), half), :].astype(bf16)
        keep[k] = product[pl.ds(pl.multiple_of(core * half, 16), half), :]


def late(at, rows, inner, outer, scale, gain, gate_weight, up_weight, sums):
    size, width = inner.shape
    cols = gate_weight.shape[1]
    half, tile = size // 2, cols // 3
    block = pl.BlockSpec((width, tile), lambda j, at: (3 - 3 * at[SIDE], j))
    away = pl.BlockSpec((half, tile), lambda j, at: (0, j))
    return kernel_call(
        functools.partial(late_kernel, rows),
        cols // tile,
        [whole(size, width)] * 2
        + [whole(*scale.shape), whole(*gain.shape), block, block]
        + [pl.BlockSpec((2, size, tile), lambda j, at: (0, 0, j))],
        [away, away, pl.BlockSpec((2, half, tile), lambda j, at: (0, 0, j))],
        [((half, cols), bf16), ((half, cols), bf16), ((2, half, cols), f32)],
        [pltpu.VMEM((size, width), bf16), pltpu.VMEM((size, tile), f32)],
        "late",
    )(at, inner, outer, scale, gain, gate_weight, up_weight, sums)


def sum_kernel(at, keep, gate, up, share, mine):
    x, part = at[X], share.shape[1]
    for k, come in enumerate((gate, up)):
        for quarter, out in ((1 - x, share), (x, mine)):
            rows = pl.ds(pl.multiple_of(quarter * part, 16), part)
            out[k] = (keep[k, rows, :] + come[rows, :].astype(f32)).astype(out.dtype)


def add_core(at, keep, gate, up):
    _, half, cols = keep.shape
    part, tile = half // 2, cols // 3
    piece = lambda *shape: pl.BlockSpec((*shape, tile), lambda j, at: (0,) * len(shape) + (j,))
    return kernel_call(
        sum_kernel,
        cols // tile,
        [piece(2, half), piece(half), piece(half)],
        [piece(2, part), piece(2, part)],
        [((2, part, cols), bf16), ((2, part, cols), f32)],
        [],
        "add_core",
    )(at, keep, gate, up)


def down_kernel(at, near, far, weight, terms, ahead, hidden):
    x = at[X]
    part = near.shape[0] // 2

    @pl.when(pl.program_id(0) == 0)
    def _():
        for core in range(2):
            for quarter, pieces in ((2 * core + x, near), (2 * core + 1 - x, far)):
                row = pl.multiple_of(quarter * part, 16)
                hidden[pl.ds(row, part), :] = pieces[core * part : (core + 1) * part, :]

    product = jnp.dot(hidden[...], weight[...], preferred_element_type=f32)
    terms[0] = product

    @pl.when(pl.program_id(0) == 3 - at[PLACE])
    def _():
        ahead[...] = product.astype(bf16)


def down(at, near, far, down_weight):
    both, depth = near.shape
    size, width = 2 * both, down_weight.shape[1] // 4
    return kernel_call(
        down_kernel,
        4,
        [whole(both, depth)] * 2 + [pl.BlockSpec((depth, width), lambda j, at: (0, j))],
        [pl.BlockSpec((1, size, width), lambda j, at: (j, 0, 0)), whole(size, width)],
        [((4, size, width), f32), ((size, width), bf16)],
        [pltpu.VMEM((size, depth), bf16)],
        "down",
    )(at, near, far, down_weight)


class Turn:
    def __init__(self):
        self.held = ()

    def take(self, *values):
        values, _ = lax.optimization_barrier((values, self.held))
        self.held = values
        return values

    def give(self, *values):
        self.held = values


def chunk_blocks(turn, at, first, size, tokens, notes, weights, outputs):
    gate_weight, up_weight, down_weight = weights
    place = at[PLACE]
    rows = slice(first, first + size)
    along = lambda value, pairs: lax.ppermute(value, "gy", pairs)

    (own,) = turn.take(tokens[rows])
    pair, inner = along(own, PAIRS), along(own, MIDDLE)
    yield
    pair, inner = turn.take(pair, inner)
    far_inner, outer = along(pair, MIDDLE), along(inner, OUTWARD)
    yield
    far_inner, outer = turn.take(far_inner, outer)
    far_outer = along(far_inner, OUTWARD)
    yield
    own, pair, inner, outer = turn.take(own, pair, inner, outer)
    sums = early(at, rows, own, pair, inner, outer, *notes, gate_weight, up_weight)
    turn.give(sums)
    yield
    far_outer, sums = turn.take(far_outer, sums)
    *send, keep = late(at, rows, far_inner, far_outer, *notes, gate_weight, up_weight, sums)
    turn.give(*send, keep)

    come = [lax.ppermute(value, "gx", SWAP_CORE) for value in send]
    yield
    *come, keep = turn.take(*come, keep)
    share, mine = add_core(at, keep, *come)
    turn.give(share, mine)
    come = lax.ppermute(share, "gx", SWAP_X)
    yield
    come, mine = turn.take(come, mine)
    mine = mine + come.astype(f32)
    hidden = (jax.nn.silu(mine[0]) * mine[1]).astype(bf16)
    turn.give(hidden)
    cores = lambda value: lax.all_gather(value, "gx", axis_index_groups=[[0, 1], [2, 3]], axis=0, tiled=True)
    far, near = lax.ppermute(hidden, "gx", SWAP_X), cores(hidden)
    yield
    far, near = turn.take(far, near)
    terms, ahead = down(at, near, cores(far), down_weight)
    turn.give(ahead)

    pick = lambda j: lax.dynamic_index_in_dim(terms, j, 0, keepdims=False)
    from_end = along(ahead, INWARD)
    yield
    (from_end,) = turn.take(from_end)
    second = (pick((place + 2) % 4) + from_end.astype(f32)).astype(bf16)
    turn.give(second)
    to_middle, to_far = along(second, INWARD), along(second, MIDDLE)
    yield
    to_middle, to_far = turn.take(to_middle, to_far)
    third = (pick(at[TWIN]) + to_far.astype(f32)).astype(bf16)
    fourth = (pick(3 - place) + to_middle.astype(f32)).astype(bf16)
    turn.give(third, fourth)
    third, fourth = along(third, PAIRS), along(fourth, MIDDLE)
    yield
    third, fourth = turn.take(third, fourth)
    total = (pick(place) + third.astype(f32) + fourth.astype(f32)).astype(bf16)
    turn.give(total)
    outputs[first] = total


def note_blocks(turn, tokens, norm_gain, notes):
    rows = tokens.shape[0]
    (values,) = turn.take(tokens)
    values = values.astype(f32)
    squares = jnp.sum(values * values, axis=1)
    turn.give(squares)
    other = lax.ppermute(squares, "gx", SWAP_CORE)
    yield
    squares, other = turn.take(squares, other)
    squares = squares + other
    turn.give(squares)
    other = lax.ppermute(squares, "gx", SWAP_X)
    yield
    squares, other = turn.take(squares, other)
    note = jnp.concatenate([squares + other, norm_gain.astype(f32)])
    turn.give(note)
    found = [note] + [lax.ppermute(note, "gy", [(j, (j + t) % 4) for j in range(4)]) for t in range(1, 4)]
    yield
    found = turn.take(*found)
    scale = lax.rsqrt(sum(note[:rows] for note in found) / D + epsilon)[:, None]
    gain = jnp.stack([note[rows:] for note in found])
    turn.give(scale, gain)
    notes.extend((scale, gain))


def chunked(tokens, norm_gain, *weights):
    place, index = lax.axis_index("gy"), lax.axis_index("gx")
    at = jnp.stack([place, index % 2, index // 2, place // 2, place + 1 - 2 * (place % 2)]).astype(jnp.int32)
    turn, notes, outputs = Turn(), [], {}
    chunks, first = [], 0
    for size in CHUNKS:
        chunks.append(chunk_blocks(turn, at, first, size, tokens, notes, weights, outputs))
        first += size
    noting = note_blocks(turn, tokens, norm_gain, notes)
    for blocks in (chunks[0], noting, noting, chunks[0], noting, chunks[0], noting):
        next(blocks, None)
    for c in ORDER:
        next(chunks[c], None)
    return jnp.concatenate([outputs[f] for f in sorted(outputs)])


def plain(tokens, norm_gain, gate_weight, up_weight, down_weight):
    values = tokens.astype(f32)
    squares = lax.psum(jnp.sum(values * values, axis=1), ("gx", "gy"))
    normed = (
        values * lax.rsqrt(squares / D + epsilon)[:, None] * norm_gain.astype(f32)[None, :]
    ).astype(bf16)
    gathered = lax.all_gather(normed, "gy", axis=1, tiled=True)
    gate, up = (
        lax.psum_scatter(
            jnp.dot(gathered, weight, preferred_element_type=f32), "gx", scatter_dimension=1, tiled=True
        )
        for weight in (gate_weight, up_weight)
    )
    hidden = (jax.nn.silu(gate) * up).astype(bf16)
    terms = jnp.dot(
        lax.all_gather(hidden, "gx", axis=1, tiled=True), down_weight, preferred_element_type=f32
    )
    return lax.psum_scatter(terms, "gy", scatter_dimension=1, tiled=True).astype(bf16)


def local(sizes, tokens, *rest):
    micro_count, row_count, width = tokens.shape
    rows = micro_count * row_count
    form = chunked if sizes == (4, 4) and rows == sum(CHUNKS) and width % 128 == 0 else plain
    return form(tokens.reshape(rows, width), *rest).reshape(tokens.shape)


def solution(mesh):
    in_specs = (
        P(None, "groups", ("gx", "gy")),
        P(("gx", "gy")),
        P("gx", "gy"),
        P("gx", "gy"),
        P("gy", "gx"),
    )
    out_specs = P(None, "groups", ("gx", "gy"))
    return jax.shard_map(
        functools.partial(local, (mesh.shape["gx"], mesh.shape["gy"])),
        mesh=mesh,
        in_specs=in_specs,
        out_specs=out_specs,
        check_vma=False,
    )
```

time: 796 us -> 393 us (0.49)
  waiting for transfers between devices: 642 us -> 111 us
  Pallas kernels: 0 us -> 151 us
  matrix products: 90.1 us -> 0 us
  starting transfers between devices: 0.57 us -> 87.5 us
  blocking collectives: 35.1 us -> 15.7 us
  between operations: 13.1 us -> 0.63 us
  local copies, waits for them, and re-layouts: 0.01 us -> 11.8 us
    reduce_scatter x3 -> x0, waiting for transfers between devices: 441 us -> none  [the longest x1 314 us: layer_block(): lax.psum_scatter(terms, 'gy', scatter_dimension=1, tiled=True)]
    all_gather x2 -> x0, waiting for transfers between devices: 201 us -> none  [the longest x1 164 us: layer_block(): shard_piece = lax.all_gather(normed, 'gy', axis=1, tiled=True)]
    pallas_call x0 -> x12, Pallas kernels: none -> 151 us  [the longest x3 64.2 us: early(): kernel_call(functools.partial(early_kernel, rows), cols // tile, [whole(s...]
    ppermute x0 -> x47, waiting for transfers between devices: none -> 111 us  [the longest x30 103 us: chunk_blocks(): along = lambda value, pairs: lax.ppermute(value, 'gy', pairs)]
    dot_general x3 -> x0, matrix products: 90.1 us -> none  [the longest x1 30.9 us: layer_block(): up_sum = jnp.dot(shard_piece, up_weight, preferred_element_type=jnp.float32)]
    ppermute x0 -> x47, starting transfers between devices: none -> 87.5 us  [the longest x30 70.5 us: chunk_blocks(): along = lambda value, pairs: lax.ppermute(value, 'gy', pairs)]
    psum x1 -> x0, blocking collectives: 35.1 us -> none  [layer_block(): squares = lax.psum(jnp.sum(values * values, axis=1), ('gx', 'gy'))]
    all_gather x0 -> x6, blocking collectives: none -> 15.7 us  [chunk_blocks(): lax.all_gather(value, 'gx', axis_index_groups=[[0, 1], [2, 3]], axis=0, t...]
  transfers between devices with their start and end apart: 5 -> 47, of which waited for: 5 -> 15; matrix products, arithmetic and copies ran while one was open for 4% -> 3% of each run, Pallas kernels for 0% -> 35%
where the time goes in v2:
time: 393 us; the launch traced here: 391 us
  Pallas kernels  151 us (38%)
  waiting for transfers between devices  111 us (28%)
  starting transfers between devices  87.5 us (22%)
  blocking collectives  15.7 us (4%)
  other arithmetic  13.3 us (3%)
  local copies, waits for them, and re-layouts  11.8 us (3%)
    ppermute x30, waiting for transfers between devices, chunk_blocks(): along = lambda value, pairs: lax.ppermute(value, 'gy', pairs)  103 us
    ppermute x30, starting transfers between devices, chunk_blocks(): along = lambda value, pairs: lax.ppermute(value, 'gy', pairs)  70.5 us
    pallas_call x3, Pallas kernels, early(): kernel_call(functools.partial(early_kernel, rows), cols // tile, [whole(s...  64.2 us
    pallas_call x3, Pallas kernels, down(): kernel_call(down_kernel, 4, [whole(both, depth)] * 2 + [pl.BlockSpec((dep...  43.7 us
    pallas_call x3, Pallas kernels, late(): kernel_call(functools.partial(late_kernel, rows), cols // tile, [whole(si...  34.3 us
    all_gather x6, blocking collectives, chunk_blocks(): lax.all_gather(value, 'gx', axis_index_groups=[[0, 1], [2, 3]], axis=0, t...  15.7 us
    pallas_call x3, Pallas kernels, add_core(): kernel_call(sum_kernel, cols // tile, [piece(2, half), piece(half), piece...  8.97 us
    unnamed x30, local copies, waits for them, and re-layouts  8.6 us
  transfers between devices with their start and end apart: 47, of which 15 were waited for; matrix products, arithmetic and copies ran while one was open for 3% of the time, Pallas kernels for 35%

profile of v2, /device:TPU:0, one launch (start us, length us, event | category | flops | bytes accessed | tf_op | source)
XLA Modules:
  0.0 391.0 jit_solution(15191057114188747271)
XLA Ops:
  2.5 5.9 %collective-permute-start = (bf16[384,1152]{1,0:T(8,128)(2,1)S(1)}, bf16[384,1152]{1,0:T(8,128)(2,1)S(1)}, u32[]{:S(2)}, u32[]{:S(2)}) collective-permute-start(bf16[384,1152]{1,0:T(8,128)(2,1)S(1)} %get-tuple-element.117.own), channel_id=1, source_target_pairs={{0,1},{1,0},{2,3},{3,2},{4,5},{5,4},{6,7},{7,6},{8,9},{9,8},{10,11... | collective-permute-start | bytes 2654216 | tf_op jit(solution)/shard_map/ppermute | solution.py:202
  10.1 17.6 %collective-permute-done.pair = bf16[384,1152]{1,0:T(8,128)(2,1)S(1)} collective-permute-done((bf16[384,1152]{1,0:T(8,128)(2,1)S(1)}, bf16[384,1152]{1,0:T(8,128)(2,1)S(1)}, u32[]{:S(2)}, u32[]{:S(2)}) %collective-permute-start) | collective-permute-done | bytes 884768 | tf_op jit(solution)/shard_map/ppermute | solution.py:202
  36.6 3.5 collective-permute-start.8
  41.7 11.1 %collective-permute-done.4.outer = bf16[384,1152]{1,0:T(8,128)(2,1)S(1)} collective-permute-done((bf16[384,1152]{1,0:T(8,128)(2,1)S(1)}, bf16[384,1152]{1,0:T(8,128)(2,1)S(1)}, u32[]{:S(2)}, u32[]{:S(2)}) %collective-permute-start.4) | collective-permute-done | bytes 884768 | tf_op jit(solution)/shard_map/ppermute | solution.py:202
  62.1 22.1 %early.3.sums = f32[2,384,2304]{2,1,0:T(8,128)} custom-call(s32[5]{0:T(128)S(1)} %stack.38.at, bf16[384,1152]{1,0:T(8,128)(2,1)S(1)} %get-tuple-element.117.own, bf16[384,1152]{1,0:T(8,128)(2,1)S(1)} %copy-done.5, bf16[384,1152]{1,0:T(8,128)(2,1)S(1)} %copy-done.3, bf16[384,1152]{1,0:T(8,128)(2,1)S(1)} %copy-done.7, f32[1024,1]{1,0:T(8,128)S(1)} %copy.6.scale, ...), custom_call_target="tpu_custom_call" | custom-call | tf_op jit(solution)/shard_map/early/pallas_call | solution.py:82
  84.2 9.5 %collective-permute-done.6.outer = bf16[384,1152]{1,0:T(8,128)(2,1)} collective-permute-done((bf16[384,1152]{1,0:T(8,128)(2,1)S(1)}, bf16[384,1152]{1,0:T(8,128)(2,1)}, u32[]{:S(2)}, u32[]{:S(2)}) %collective-permute-start.6) | collective-permute-done | bytes 884768 | tf_op jit(solution)/shard_map/ppermute | solution.py:202
  93.7 12.8 %late.3 = (bf16[192,2304]{1,0:T(8,128)(2,1)S(1)}, bf16[192,2304]{1,0:T(8,128)(2,1)S(1)}, f32[2,192,2304]{2,1,0:T(8,128)}) custom-call(s32[5]{0:T(128)S(1)} %stack.38.at, bf16[384,1152]{1,0:T(8,128)(2,1)S(1)} %collective-permute-done.3.inner, bf16[384,1152]{1,0:T(8,128)(2,1)} %collective-permute-done.6.outer, f32[1024,1]{1,0:T(8,128)S(1)} %copy.6.scale, ...), custom_call_target="tpu_custom_call" | custom-call | tf_op jit(solution)/shard_map/late/pallas_call | solution.py:116
  110.3 3.5 add_core.3
  117.1 4.3 %collective-permute-start.19 = (bf16[256,1152]{1,0:T(8,128)(2,1)S(1)}, bf16[256,1152]{1,0:T(8,128)(2,1)S(1)}, u32[]{:S(2)}, u32[]{:S(2)}) collective-permute-start(bf16[256,1152]{1,0:T(8,128)(2,1)S(1)} %slice.70.own), channel_id=1, source_target_pairs={{0,1},{1,0},{2,3},{3,2},{4,5},{5,4},{6,7},{7,6},{8,9},{9,8},{10,11... | collective-permute-start | bytes 1769480 | tf_op jit(solution)/shard_map/ppermute | solution.py:202
  121.4 11.0 %collective-permute-done.16.outer = bf16[384,1152]{1,0:T(8,128)(2,1)S(1)} collective-permute-done((bf16[384,1152]{1,0:T(8,128)(2,1)}, bf16[384,1152]{1,0:T(8,128)(2,1)S(1)}, u32[]{:S(2)}, u32[]{:S(2)}) %collective-permute-start.16) | collective-permute-done | bytes 884768 | tf_op jit(solution)/shard_map/ppermute | solution.py:202
  133.7 23.1 %early.4.sums = f32[2,384,2304]{2,1,0:T(8,128)} custom-call(s32[5]{0:T(128)S(1)} %stack.38.at, bf16[384,1152]{1,0:T(8,128)(2,1)S(1)} %get-tuple-element.136.own, bf16[384,1152]{1,0:T(8,128)(2,1)} %collective-permute-done.10.pair, bf16[384,1152]{1,0:T(8,128)(2,1)} %collective-permute-done.11.inner, bf16[384,1152]{1,0:T(8,128)(2,1)S(1)} %collective-permute-done.16.outer, ...), custom_call_target="tpu_custom_call" | custom-call | tf_op jit(solution)/shard_map/early/pallas_call | solution.py:82
  163.0 12.1 %late.4 = (bf16[192,2304]{1,0:T(8,128)(2,1)S(1)}, bf16[192,2304]{1,0:T(8,128)(2,1)S(1)}, f32[2,192,2304]{2,1,0:T(8,128)}) custom-call(s32[5]{0:T(128)S(1)} %stack.38.at, bf16[384,1152]{1,0:T(8,128)(2,1)S(1)} %collective-permute-done.15.inner, bf16[384,1152]{1,0:T(8,128)(2,1)S(1)} %collective-permute-done.18.outer, f32[1024,1]{1,0:T(8,128)S(1)} %copy.6.scale, ...), custom_call_target="tpu_custom_call" | custom-call | tf_op jit(solution)/shard_map/late/pallas_call | solution.py:116
  175.7 3.8 all_gather.18.near
  181.9 15.5 %down.3 = (f32[4,384,1152]{2,1,0:T(8,128)}, bf16[384,1152]{1,0:T(8,128)(2,1)}) custom-call(s32[5]{0:T(128)S(1)} %stack.38.at, bf16[192,2304]{1,0:T(8,128)(2,1)S(1)} %all_gather.18.near, bf16[192,2304]{1,0:T(8,128)(2,1)S(1)} %all_gather.19.far, bf16[2304,4608]{1,0:T(8,128)(2,1)} %weight.5), custom_call_target="tpu_custom_call" | custom-call | tf_op jit(solution)/shard_map/down/pallas_call | solution.py:174
  197.4 6.0 %collective-permute-start.21 = (bf16[384,1152]{1,0:T(8,128)(2,1)}, bf16[384,1152]{1,0:T(8,128)(2,1)}, u32[]{:S(2)}, u32[]{:S(2)}) collective-permute-start(bf16[384,1152]{1,0:T(8,128)(2,1)} %get-tuple-element.152), channel_id=1, source_target_pairs={{0,1},{3,2},{4,5},{7,6},{8,9},{11,10},{12,13},{15,14},{16,17},{19,... | collective-permute-start | bytes 2654216 | tf_op jit(solution)/shard_map/ppermute | solution.py:202
  203.4 4.3 %add_core.4 = (bf16[2,96,2304]{2,1,0:T(8,128)(2,1)}, f32[2,96,2304]{2,1,0:T(8,128)S(1)}) custom-call(s32[5]{0:T(128)S(1)} %stack.38.at, f32[2,192,2304]{2,1,0:T(8,128)} %get-tuple-element.155.keep, bf16[192,2304]{1,0:T(8,128)(2,1)S(1)} %collective-permute-done.24.gate, bf16[192,2304]{1,0:T(8,128)(2,1)S(1)} %collective-permute-done.25.up), custom_call_target="tpu_custom_call" | custom-call | tf_op jit(solution)/shard_map/add_core/pallas_call | solution.py:141
  211.9 19.0 %early.5.sums = f32[2,256,2304]{2,1,0:T(8,128)} custom-call(s32[5]{0:T(128)S(1)} %stack.38.at, bf16[256,1152]{1,0:T(8,128)(2,1)S(1)} %slice.70.own, bf16[256,1152]{1,0:T(8,128)(2,1)S(1)} %collective-permute-done.19.pair, bf16[256,1152]{1,0:T(8,128)(2,1)S(1)} %collective-permute-done.20.inner, bf16[256,1152]{1,0:T(8,128)(2,1)S(1)} %copy-done.9, ...), custom_call_target="tpu_custom_call" | custom-call | tf_op jit(solution)/shard_map/early/pallas_call | solution.py:82
  233.7 7.2 %collective-permute-start.26 = (bf16[384,1152]{1,0:T(8,128)(2,1)S(1)}, bf16[384,1152]{1,0:T(8,128)(2,1)S(1)}, u32[]{:S(2)}, u32[]{:S(2)}) collective-permute-start(bf16[384,1152]{1,0:T(8,128)(2,1)S(1)} %fusion.6), channel_id=1, source_target_pairs={{0,1},{3,2},{4,5},{7,6},{8,9},{11,10},{12,13},{15,14},{16,17},{19,... | collective-permute-start | bytes 2654216 | tf_op jit(solution)/shard_map/ppermute | solution.py:202
  240.9 9.4 %late.5 = (bf16[128,2304]{1,0:T(8,128)(2,1)S(1)}, bf16[128,2304]{1,0:T(8,128)(2,1)S(1)}, f32[2,128,2304]{2,1,0:T(8,128)S(1)}) custom-call(s32[5]{0:T(128)S(1)} %stack.38.at, bf16[256,1152]{1,0:T(8,128)(2,1)} %collective-permute-done.22.inner, bf16[256,1152]{1,0:T(8,128)(2,1)} %collective-permute-done.28.outer, f32[1024,1]{1,0:T(8,128)S(1)} %copy.6.scale, ...), custom_call_target="tpu_custom_call" | custom-call | tf_op jit(solution)/shard_map/late/pallas_call | solution.py:116
  262.1 5.1 %collective-permute-start.32 = (bf16[384,1152]{1,0:T(8,128)(2,1)S(1)}, bf16[384,1152]{1,0:T(8,128)(2,1)S(1)}, u32[]{:S(2)}, u32[]{:S(2)}) collective-permute-start(bf16[384,1152]{1,0:T(8,128)(2,1)S(1)} %get-tuple-element.204), channel_id=1, source_target_pairs={{0,1},{1,0},{2,3},{3,2},{4,5},{5,4},{6,7},{7,6},{8,9},{9,8},{10,11... | collective-permute-start | bytes 2654216 | tf_op jit(solution)/shard_map/ppermute | solution.py:202
  269.7 15.2 %down.4 = (f32[4,384,1152]{2,1,0:T(8,128)}, bf16[384,1152]{1,0:T(8,128)(2,1)S(1)}) custom-call(s32[5]{0:T(128)S(1)} %stack.38.at, bf16[192,2304]{1,0:T(8,128)(2,1)S(1)} %all_gather.20.near, bf16[192,2304]{1,0:T(8,128)(2,1)S(1)} %all_gather.21.far, bf16[2304,4608]{1,0:T(8,128)(2,1)} %weight.5), custom_call_target="tpu_custom_call" | custom-call | tf_op jit(solution)/shard_map/down/pallas_call | solution.py:174
  292.8 3.3 collective-permute-done.37
  298.4 13.1 %down.5 = (f32[4,256,1152]{2,1,0:T(8,128)}, bf16[256,1152]{1,0:T(8,128)(2,1)S(1)}) custom-call(s32[5]{0:T(128)S(1)} %stack.38.at, bf16[128,2304]{1,0:T(8,128)(2,1)S(1)} %all_gather.22.near, bf16[128,2304]{1,0:T(8,128)(2,1)S(1)} %all_gather.23.far, bf16[2304,4608]{1,0:T(8,128)(2,1)} %weight.5), custom_call_target="tpu_custom_call" | custom-call | tf_op jit(solution)/shard_map/down/pallas_call | solution.py:174
  314.0 3.2 collective-permute-start.38
  317.2 9.4 %collective-permute-done.40 = bf16[256,1152]{1,0:T(8,128)(2,1)S(1)} collective-permute-done((bf16[256,1152]{1,0:T(8,128)(2,1)S(1)}, bf16[256,1152]{1,0:T(8,128)(2,1)S(1)}, u32[]{:S(2)}, u32[]{:S(2)}) %collective-permute-start.40) | collective-permute-done | bytes 589856 | tf_op jit(solution)/shard_map/ppermute | solution.py:202
  328.9 6.5 %collective-permute-start.43 = (bf16[256,1152]{1,0:T(8,128)(2,1)S(1)}, bf16[256,1152]{1,0:T(8,128)(2,1)S(1)}, u32[]{:S(2)}, u32[]{:S(2)}) collective-permute-start(bf16[256,1152]{1,0:T(8,128)(2,1)S(1)} %fusion.14), channel_id=1, source_target_pairs={{0,1},{3,2},{4,5},{7,6},{8,9},{11,10},{12,13},{15,14},{16,17},{19,... | collective-permute-start | bytes 1769480 | tf_op jit(solution)/shard_map/ppermute | solution.py:202
  335.4 10.2 %collective-permute-done.38 = bf16[384,1152]{1,0:T(8,128)(2,1)S(1)} collective-permute-done((bf16[384,1152]{1,0:T(8,128)(2,1)S(1)}, bf16[384,1152]{1,0:T(8,128)(2,1)S(1)}, u32[]{:S(2)}, u32[]{:S(2)}) %collective-permute-start.38) | collective-permute-done | bytes 884768 | tf_op jit(solution)/shard_map/ppermute | solution.py:202
  346.7 4.4 %collective-permute-start.41 = (bf16[384,1152]{1,0:T(8,128)(2,1)S(1)}, bf16[384,1152]{1,0:T(8,128)(2,1)S(1)}, u32[]{:S(2)}, u32[]{:S(2)}) collective-permute-start(bf16[384,1152]{1,0:T(8,128)(2,1)S(1)} %get-tuple-element.202), channel_id=1, source_target_pairs={{0,1},{1,0},{2,3},{3,2},{4,5},{5,4},{6,7},{7,6},{8,9},{9,8},{10,11... | collective-permute-start | bytes 2654216 | tf_op jit(solution)/shard_map/ppermute | solution.py:202
  351.2 7.1 %collective-permute-done.43 = bf16[256,1152]{1,0:T(8,128)(2,1)S(1)} collective-permute-done((bf16[256,1152]{1,0:T(8,128)(2,1)S(1)}, bf16[256,1152]{1,0:T(8,128)(2,1)S(1)}, u32[]{:S(2)}, u32[]{:S(2)}) %collective-permute-start.43) | collective-permute-done | bytes 589856 | tf_op jit(solution)/shard_map/ppermute | solution.py:202
  359.2 4.5 %collective-permute-start.45 = (bf16[256,1152]{1,0:T(8,128)(2,1)S(1)}, bf16[256,1152]{1,0:T(8,128)(2,1)S(1)}, u32[]{:S(2)}, u32[]{:S(2)}) collective-permute-start(bf16[256,1152]{1,0:T(8,128)(2,1)S(1)} %get-tuple-element.206), channel_id=1, source_target_pairs={{0,1},{1,0},{2,3},{3,2},{4,5},{5,4},{6,7},{7,6},{8,9},{9,8},{10,11... | collective-permute-start | bytes 1769480 | tf_op jit(solution)/shard_map/ppermute | solution.py:202
  363.7 13.6 %collective-permute-done.41 = bf16[384,1152]{1,0:T(8,128)(2,1)S(1)} collective-permute-done((bf16[384,1152]{1,0:T(8,128)(2,1)S(1)}, bf16[384,1152]{1,0:T(8,128)(2,1)S(1)}, u32[]{:S(2)}, u32[]{:S(2)}) %collective-permute-start.41) | collective-permute-done | bytes 884768 | tf_op jit(solution)/shard_map/ppermute | solution.py:202
  377.6 11.6 %collective-permute-done.45 = bf16[256,1152]{1,0:T(8,128)(2,1)S(1)} collective-permute-done((bf16[256,1152]{1,0:T(8,128)(2,1)S(1)}, bf16[256,1152]{1,0:T(8,128)(2,1)S(1)}, u32[]{:S(2)}, u32[]{:S(2)}) %collective-permute-start.45) | collective-permute-done | bytes 589856 | tf_op jit(solution)/shard_map/ppermute | solution.py:202
  (146 shorter events, 81.4 us)
Async XLA Ops:
  2.5 25.2 %collective-permute-start = (bf16[384,1152]{1,0:T(8,128)(2,1)S(1)}, bf16[384,1152]{1,0:T(8,128)(2,1)S(1)}, u32[]{:S(2)}, u32[]{:S(2)}) collective-permute-start(bf16[384,1152]{1,0:T(8,128)(2,1)S(1)} %get-tuple-element.117.own), channel_id=1, source_target_pairs={{0,1},{1,0},{2,3},{3,2},{4,5},{5,4},{6,7},{7,6},{8,9},{9,8},{10,11... | collective-permute-start | bytes 2654216 | tf_op jit(solution)/shard_map/ppermute | solution.py:202
  29.3 23.5 %collective-permute-start.4 = (bf16[384,1152]{1,0:T(8,128)(2,1)S(1)}, bf16[384,1152]{1,0:T(8,128)(2,1)S(1)}, u32[]{:S(2)}, u32[]{:S(2)}) collective-permute-start(bf16[384,1152]{1,0:T(8,128)(2,1)S(1)} %collective-permute-done.1.inner), channel_id=1, source_target_pairs={{1,0},{2,3},{5,4},{6,7},{9,8},{10,11},{13,12},{14,15},{17,16},{18,... | collective-permute-start | bytes 2654216 | tf_op jit(solution)/shard_map/ppermute | solution.py:202
  35.2 18.6 %collective-permute-start.9 = (f32[2176]{0:T(1024)S(1)}, f32[2176]{0:T(1024)S(1)}, u32[]{:S(2)}, u32[]{:S(2)}) collective-permute-start(f32[2176]{0:T(1024)S(1)} %pad_maximum_fusion.2), channel_id=1, source_target_pairs={{0,3},{1,0},{2,1},{3,2},{4,7},{5,4},{6,5},{7,6},{8,11},{9,8},{10,9... | collective-permute-start | bytes 26120 | tf_op jit(solution)/shard_map/ppermute | solution.py:275
  53.9 30.3 %collective-permute-start.11 = (bf16[384,1152]{1,0:T(8,128)(2,1)S(1)}, bf16[384,1152]{1,0:T(8,128)(2,1)}, u32[]{:S(2)}, u32[]{:S(2)}) collective-permute-start(bf16[384,1152]{1,0:T(8,128)(2,1)S(1)} %get-tuple-element.136.own), channel_id=1, source_target_pairs={{1,2},{2,1},{5,6},{6,5},{9,10},{10,9},{13,14},{14,13},{17,18},{18,... | collective-permute-start | bytes 2654216 | tf_op jit(solution)/shard_map/ppermute | solution.py:202
  55.6 28.6 %collective-permute-start.10 = (bf16[384,1152]{1,0:T(8,128)(2,1)S(1)}, bf16[384,1152]{1,0:T(8,128)(2,1)}, u32[]{:S(2)}, u32[]{:S(2)}) collective-permute-start(bf16[384,1152]{1,0:T(8,128)(2,1)S(1)} %get-tuple-element.136.own), channel_id=1, source_target_pairs={{0,1},{1,0},{2,3},{3,2},{4,5},{5,4},{6,7},{7,6},{8,9},{9,8},{10,11... | collective-permute-start | bytes 2654216 | tf_op jit(solution)/shard_map/ppermute | solution.py:202
  57.0 36.8 %collective-permute-start.6 = (bf16[384,1152]{1,0:T(8,128)(2,1)S(1)}, bf16[384,1152]{1,0:T(8,128)(2,1)}, u32[]{:S(2)}, u32[]{:S(2)}) collective-permute-start(bf16[384,1152]{1,0:T(8,128)(2,1)S(1)} %collective-permute-done.3.inner), channel_id=1, source_target_pairs={{1,0},{2,3},{5,4},{6,7},{9,8},{10,11},{13,12},{14,15},{17,16},{18,... | collective-permute-start | bytes 2654216 | tf_op jit(solution)/shard_map/ppermute | solution.py:202
  107.8 24.6 %collective-permute-start.16 = (bf16[384,1152]{1,0:T(8,128)(2,1)}, bf16[384,1152]{1,0:T(8,128)(2,1)S(1)}, u32[]{:S(2)}, u32[]{:S(2)}) collective-permute-start(bf16[384,1152]{1,0:T(8,128)(2,1)} %collective-permute-done.11.inner), channel_id=1, source_target_pairs={{1,0},{2,3},{5,4},{6,7},{9,8},{10,11},{13,12},{14,15},{17,16},{18,... | collective-permute-start | bytes 2654216 | tf_op jit(solution)/shard_map/ppermute | solution.py:202
  113.7 43.0 %collective-permute-start.14 = (bf16[2,96,2304]{2,1,0:T(8,128)(2,1)S(1)}, bf16[2,96,2304]{2,1,0:T(8,128)(2,1)S(1)}, u32[]{:S(2)}, u32[]{:S(2)}) collective-permute-start(bf16[2,96,2304]{2,1,0:T(8,128)(2,1)S(1)} %get-tuple-element.131), channel_id=1, source_target_pairs={{0,8},{4,12},{8,0},{12,4},{1,9},{5,13},{9,1},{13,5},{2,10},{6,14},... | collective-permute-start | bytes 2654216 | tf_op jit(solution)/shard_map/ppermute | solution.py:226
  116.4 42.3 %collective-permute-start.20 = (bf16[256,1152]{1,0:T(8,128)(2,1)S(1)}, bf16[256,1152]{1,0:T(8,128)(2,1)S(1)}, u32[]{:S(2)}, u32[]{:S(2)}) collective-permute-start(bf16[256,1152]{1,0:T(8,128)(2,1)S(1)} %slice.70.own), channel_id=1, source_target_pairs={{1,2},{2,1},{5,6},{6,5},{9,10},{10,9},{13,14},{14,13},{17,18},{18,... | collective-permute-start | bytes 1769480 | tf_op jit(solution)/shard_map/ppermute | solution.py:202
  117.1 41.6 %collective-permute-start.19 = (bf16[256,1152]{1,0:T(8,128)(2,1)S(1)}, bf16[256,1152]{1,0:T(8,128)(2,1)S(1)}, u32[]{:S(2)}, u32[]{:S(2)}) collective-permute-start(bf16[256,1152]{1,0:T(8,128)(2,1)S(1)} %slice.70.own), channel_id=1, source_target_pairs={{0,1},{1,0},{2,3},{3,2},{4,5},{5,4},{6,7},{7,6},{8,9},{9,8},{10,11... | collective-permute-start | bytes 1769480 | tf_op jit(solution)/shard_map/ppermute | solution.py:202
  132.4 30.6 %collective-permute-start.18 = (bf16[384,1152]{1,0:T(8,128)(2,1)S(1)}, bf16[384,1152]{1,0:T(8,128)(2,1)S(1)}, u32[]{:S(2)}, u32[]{:S(2)}) collective-permute-start(bf16[384,1152]{1,0:T(8,128)(2,1)S(1)} %collective-permute-done.15.inner), channel_id=1, source_target_pairs={{1,0},{2,3},{5,4},{6,7},{9,8},{10,11},{13,12},{14,15},{17,16},{18,... | collective-permute-start | bytes 2654216 | tf_op jit(solution)/shard_map/ppermute | solution.py:202
  157.2 22.3 %collective-permute-start.17 = (bf16[96,2304]{1,0:T(8,128)(2,1)S(1)}, bf16[96,2304]{1,0:T(8,128)(2,1)S(1)}, u32[]{:S(2)}, u32[]{:S(2)}) collective-permute-start(bf16[96,2304]{1,0:T(8,128)(2,1)S(1)} %fusion.18), channel_id=1, source_target_pairs={{0,8},{4,12},{8,0},{12,4},{1,9},{5,13},{9,1},{13,5},{2,10},{6,14},... | collective-permute-start | bytes 1327112 | tf_op jit(solution)/shard_map/ppermute | solution.py:233
  158.7 44.7 %collective-permute-start.22 = (bf16[256,1152]{1,0:T(8,128)(2,1)S(1)}, bf16[256,1152]{1,0:T(8,128)(2,1)}, u32[]{:S(2)}, u32[]{:S(2)}) collective-permute-start(bf16[256,1152]{1,0:T(8,128)(2,1)S(1)} %collective-permute-done.19.pair), channel_id=1, source_target_pairs={{1,2},{2,1},{5,6},{6,5},{9,10},{10,9},{13,14},{14,13},{17,18},{18,... | collective-permute-start | bytes 1769480 | tf_op jit(solution)/shard_map/ppermute | solution.py:202
  160.2 43.2 %collective-permute-start.23 = (bf16[256,1152]{1,0:T(8,128)(2,1)S(1)}, bf16[256,1152]{1,0:T(8,128)(2,1)S(1)}, u32[]{:S(2)}, u32[]{:S(2)}) collective-permute-start(bf16[256,1152]{1,0:T(8,128)(2,1)S(1)} %collective-permute-done.20.inner), channel_id=1, source_target_pairs={{1,0},{2,3},{5,4},{6,7},{9,8},{10,11},{13,12},{14,15},{17,16},{18,... | collective-permute-start | bytes 1769480 | tf_op jit(solution)/shard_map/ppermute | solution.py:202
  175.2 28.3 %collective-permute-start.24 = (bf16[192,2304]{1,0:T(8,128)(2,1)S(1)}, bf16[192,2304]{1,0:T(8,128)(2,1)S(1)}, u32[]{:S(2)}, u32[]{:S(2)}) collective-permute-start(bf16[192,2304]{1,0:T(8,128)(2,1)S(1)} %get-tuple-element.146), channel_id=1, source_target_pairs={{0,4},{4,0},{8,12},{12,8},{1,5},{5,1},{9,13},{13,9},{2,6},{6,2},{1... | collective-permute-start | bytes 2654216 | tf_op jit(solution)/shard_map/ppermute | solution.py:221
  175.2 28.3 %collective-permute-start.25 = (bf16[192,2304]{1,0:T(8,128)(2,1)S(1)}, bf16[192,2304]{1,0:T(8,128)(2,1)S(1)}, u32[]{:S(2)}, u32[]{:S(2)}) collective-permute-start(bf16[192,2304]{1,0:T(8,128)(2,1)S(1)} %get-tuple-element.147), channel_id=1, source_target_pairs={{0,4},{4,0},{8,12},{12,8},{1,5},{5,1},{9,13},{13,9},{2,6},{6,2},{1... | collective-permute-start | bytes 2654216 | tf_op jit(solution)/shard_map/ppermute | solution.py:221
  197.4 33.5 %collective-permute-start.21 = (bf16[384,1152]{1,0:T(8,128)(2,1)}, bf16[384,1152]{1,0:T(8,128)(2,1)}, u32[]{:S(2)}, u32[]{:S(2)}) collective-permute-start(bf16[384,1152]{1,0:T(8,128)(2,1)} %get-tuple-element.152), channel_id=1, source_target_pairs={{0,1},{3,2},{4,5},{7,6},{8,9},{11,10},{12,13},{15,14},{16,17},{19,... | collective-permute-start | bytes 2654216 | tf_op jit(solution)/shard_map/ppermute | solution.py:202
  209.0 41.9 %collective-permute-start.31 = (bf16[2,96,2304]{2,1,0:T(8,128)(2,1)}, bf16[2,96,2304]{2,1,0:T(8,128)(2,1)}, u32[]{:S(2)}, u32[]{:S(2)}) collective-permute-start(bf16[2,96,2304]{2,1,0:T(8,128)(2,1)} %get-tuple-element.158), channel_id=1, source_target_pairs={{0,8},{4,12},{8,0},{12,4},{1,9},{5,13},{9,1},{13,5},{2,10},{6,14},... | collective-permute-start | bytes 2654216 | tf_op jit(solution)/shard_map/ppermute | solution.py:226
  209.5 31.4 %collective-permute-start.28 = (bf16[256,1152]{1,0:T(8,128)(2,1)}, bf16[256,1152]{1,0:T(8,128)(2,1)}, u32[]{:S(2)}, u32[]{:S(2)}) collective-permute-start(bf16[256,1152]{1,0:T(8,128)(2,1)} %collective-permute-done.22.inner), channel_id=1, source_target_pairs={{1,0},{2,3},{5,4},{6,7},{9,8},{10,11},{13,12},{14,15},{17,16},{18,... | collective-permute-start | bytes 1769480 | tf_op jit(solution)/shard_map/ppermute | solution.py:202
  232.8 25.5 %collective-permute-start.27 = (bf16[384,1152]{1,0:T(8,128)(2,1)S(1)}, bf16[384,1152]{1,0:T(8,128)(2,1)S(1)}, u32[]{:S(2)}, u32[]{:S(2)}) collective-permute-start(bf16[384,1152]{1,0:T(8,128)(2,1)S(1)} %fusion.6), channel_id=1, source_target_pairs={{1,2},{2,1},{5,6},{6,5},{9,10},{10,9},{13,14},{14,13},{17,18},{18,... | collective-permute-start | bytes 2654216 | tf_op jit(solution)/shard_map/ppermute | solution.py:202
  233.7 25.2 %collective-permute-start.26 = (bf16[384,1152]{1,0:T(8,128)(2,1)S(1)}, bf16[384,1152]{1,0:T(8,128)(2,1)S(1)}, u32[]{:S(2)}, u32[]{:S(2)}) collective-permute-start(bf16[384,1152]{1,0:T(8,128)(2,1)S(1)} %fusion.6), channel_id=1, source_target_pairs={{0,1},{3,2},{4,5},{7,6},{8,9},{11,10},{12,13},{15,14},{16,17},{19,... | collective-permute-start | bytes 2654216 | tf_op jit(solution)/shard_map/ppermute | solution.py:202
  257.7 29.3 %collective-permute-start.34 = (bf16[2,64,2304]{2,1,0:T(8,128)(2,1)S(1)}, bf16[2,64,2304]{2,1,0:T(8,128)(2,1)S(1)}, u32[]{:S(2)}, u32[]{:S(2)}) collective-permute-start(bf16[2,64,2304]{2,1,0:T(8,128)(2,1)S(1)} %get-tuple-element.175), channel_id=1, source_target_pairs={{0,8},{4,12},{8,0},{12,4},{1,9},{5,13},{9,1},{13,5},{2,10},{6,14},... | collective-permute-start | bytes 1769480 | tf_op jit(solution)/shard_map/ppermute | solution.py:226
  261.4 29.6 %collective-permute-start.33 = (bf16[384,1152]{1,0:T(8,128)(2,1)S(1)}, bf16[384,1152]{1,0:T(8,128)(2,1)S(1)}, u32[]{:S(2)}, u32[]{:S(2)}) collective-permute-start(bf16[384,1152]{1,0:T(8,128)(2,1)S(1)} %get-tuple-element.203), channel_id=1, source_target_pairs={{1,2},{2,1},{5,6},{6,5},{9,10},{10,9},{13,14},{14,13},{17,18},{18,... | collective-permute-start | bytes 2654216 | tf_op jit(solution)/shard_map/ppermute | solution.py:202
  262.1 28.9 %collective-permute-start.32 = (bf16[384,1152]{1,0:T(8,128)(2,1)S(1)}, bf16[384,1152]{1,0:T(8,128)(2,1)S(1)}, u32[]{:S(2)}, u32[]{:S(2)}) collective-permute-start(bf16[384,1152]{1,0:T(8,128)(2,1)S(1)} %get-tuple-element.204), channel_id=1, source_target_pairs={{0,1},{1,0},{2,3},{3,2},{4,5},{5,4},{6,7},{7,6},{8,9},{9,8},{10,11... | collective-permute-start | bytes 2654216 | tf_op jit(solution)/shard_map/ppermute | solution.py:202
  284.8 28.2 %collective-permute-start.36 = (bf16[384,1152]{1,0:T(8,128)(2,1)S(1)}, bf16[384,1152]{1,0:T(8,128)(2,1)S(1)}, u32[]{:S(2)}, u32[]{:S(2)}) collective-permute-start(bf16[384,1152]{1,0:T(8,128)(2,1)S(1)} %get-tuple-element.181), channel_id=1, source_target_pairs={{0,1},{3,2},{4,5},{7,6},{8,9},{11,10},{12,13},{15,14},{16,17},{19,... | collective-permute-start | bytes 2654216 | tf_op jit(solution)/shard_map/ppermute | solution.py:202
  313.3 22.1 %collective-permute-start.39 = (bf16[384,1152]{1,0:T(8,128)(2,1)S(1)}, bf16[384,1152]{1,0:T(8,128)(2,1)S(1)}, u32[]{:S(2)}, u32[]{:S(2)}) collective-permute-start(bf16[384,1152]{1,0:T(8,128)(2,1)S(1)} %fusion.1), channel_id=1, source_target_pairs={{1,2},{2,1},{5,6},{6,5},{9,10},{10,9},{13,14},{14,13},{17,18},{18,... | collective-permute-start | bytes 2654216 | tf_op jit(solution)/shard_map/ppermute | solution.py:202
  314.0 31.6 %collective-permute-start.38 = (bf16[384,1152]{1,0:T(8,128)(2,1)S(1)}, bf16[384,1152]{1,0:T(8,128)(2,1)S(1)}, u32[]{:S(2)}, u32[]{:S(2)}) collective-permute-start(bf16[384,1152]{1,0:T(8,128)(2,1)S(1)} %fusion.1), channel_id=1, source_target_pairs={{0,1},{3,2},{4,5},{7,6},{8,9},{11,10},{12,13},{15,14},{16,17},{19,... | collective-permute-start | bytes 2654216 | tf_op jit(solution)/shard_map/ppermute | solution.py:202
  328.1 23.1 %collective-permute-start.44 = (bf16[256,1152]{1,0:T(8,128)(2,1)S(1)}, bf16[256,1152]{1,0:T(8,128)(2,1)S(1)}, u32[]{:S(2)}, u32[]{:S(2)}) collective-permute-start(bf16[256,1152]{1,0:T(8,128)(2,1)S(1)} %fusion.14), channel_id=1, source_target_pairs={{1,2},{2,1},{5,6},{6,5},{9,10},{10,9},{13,14},{14,13},{17,18},{18,... | collective-permute-start | bytes 1769480 | tf_op jit(solution)/shard_map/ppermute | solution.py:202
  328.9 29.4 %collective-permute-start.43 = (bf16[256,1152]{1,0:T(8,128)(2,1)S(1)}, bf16[256,1152]{1,0:T(8,128)(2,1)S(1)}, u32[]{:S(2)}, u32[]{:S(2)}) collective-permute-start(bf16[256,1152]{1,0:T(8,128)(2,1)S(1)} %fusion.14), channel_id=1, source_target_pairs={{0,1},{3,2},{4,5},{7,6},{8,9},{11,10},{12,13},{15,14},{16,17},{19,... | collective-permute-start | bytes 1769480 | tf_op jit(solution)/shard_map/ppermute | solution.py:202
  346.7 30.5 %collective-permute-start.41 = (bf16[384,1152]{1,0:T(8,128)(2,1)S(1)}, bf16[384,1152]{1,0:T(8,128)(2,1)S(1)}, u32[]{:S(2)}, u32[]{:S(2)}) collective-permute-start(bf16[384,1152]{1,0:T(8,128)(2,1)S(1)} %get-tuple-element.202), channel_id=1, source_target_pairs={{0,1},{1,0},{2,3},{3,2},{4,5},{5,4},{6,7},{7,6},{8,9},{9,8},{10,11... | collective-permute-start | bytes 2654216 | tf_op jit(solution)/shard_map/ppermute | solution.py:202
  358.5 19.1 %collective-permute-start.46 = (bf16[256,1152]{1,0:T(8,128)(2,1)S(1)}, bf16[256,1152]{1,0:T(8,128)(2,1)S(1)}, u32[]{:S(2)}, u32[]{:S(2)}) collective-permute-start(bf16[256,1152]{1,0:T(8,128)(2,1)S(1)} %get-tuple-element.205), channel_id=1, source_target_pairs={{1,2},{2,1},{5,6},{6,5},{9,10},{10,9},{13,14},{14,13},{17,18},{18,... | collective-permute-start | bytes 1769480 | tf_op jit(solution)/shard_map/ppermute | solution.py:202
  359.2 30.0 %collective-permute-start.45 = (bf16[256,1152]{1,0:T(8,128)(2,1)S(1)}, bf16[256,1152]{1,0:T(8,128)(2,1)S(1)}, u32[]{:S(2)}, u32[]{:S(2)}) collective-permute-start(bf16[256,1152]{1,0:T(8,128)(2,1)S(1)} %get-tuple-element.206), channel_id=1, source_target_pairs={{0,1},{1,0},{2,3},{3,2},{4,5},{5,4},{6,7},{7,6},{8,9},{9,8},{10,11... | collective-permute-start | bytes 1769480 | tf_op jit(solution)/shard_map/ppermute | solution.py:202
  (30 other events, 279.7 us)

commit v3 on v2

--- a/solution.py
+++ b/solution.py
@@ -48,7 +48,7 @@
 
 
 def early_kernel(rows, at, own, pair, inner, outer, scale, gain, *refs):
-    weights, sums, normed = refs[:6], refs[6], refs[7]
+    gate_w, up_w, sums, normed = refs
     width = own.shape[1]
     place, side = at[PLACE], at[SIDE]
 
@@ -64,30 +64,26 @@
         pl.when(middle)(lambda: fill(2 - side, inner))
         pl.when(jnp.logical_not(middle))(lambda: fill(2 - side, outer))
 
-    for k in range(2):
-        total = None
-        for m in range(3):
-            term = jnp.dot(
-                normed[:, m * width : (m + 1) * width], weights[3 * k + m][...], preferred_element_type=f32
-            )
-            total = term if total is None else total + term
-        sums[k] = total
+    for k, weight in enumerate((gate_w, up_w)):
+        sums[k] = jnp.dot(normed[...], weight[...], preferred_element_type=f32)
 
 
 def early(at, rows, own, pair, inner, outer, scale, gain, gate_weight, up_weight):
     size, width = own.shape
     cols = gate_weight.shape[1]
     tile = 256
-    blocks = [pl.BlockSpec((width, tile), lambda j, at, m=m: (at[SIDE] + m, j)) for m in range(3)]
+    block = pl.BlockSpec(
+        (pl.Element(3 * width), pl.Element(tile)), lambda j, at: (at[SIDE] * width, j * tile)
+    )
     return kernel_call(
         functools.partial(early_kernel, rows),
         cols // tile,
-        [whole(size, width)] * 4 + [whole(*scale.shape), whole(*gain.shape)] + blocks * 2,
+        [whole(size, width)] * 4 + [whole(*scale.shape), whole(*gain.shape), block, block],
         [pl.BlockSpec((2, size, tile), lambda j, at: (0, 0, j))],
         [((2, size, cols), f32)],
         [pltpu.VMEM((size, 3 * width), bf16)],
         "early",
-    )(at, own, pair, inner, outer, scale, gain, *[gate_weight] * 3, *[up_weight] * 3)[0]
+    )(at, own, pair, inner, outer, scale, gain, gate_weight, up_weight)[0]
 
 
 def late_kernel(rows, at, inner, outer, scale, gain, gate_w, up_w, sums, send_gate, send_up, keep, normed, product):
@@ -110,7 +106,7 @@
 def late(at, rows, inner, outer, scale, gain, gate_weight, up_weight, sums):
     size, width = inner.shape
     cols = gate_weight.shape[1]
-    half, tile = size // 2, cols // 3
+    half, tile = size // 2, 256
     block = pl.BlockSpec((width, tile), lambda j, at: (3 - 3 * at[SIDE], j))
     away = pl.BlockSpec((half, tile), lambda j, at: (0, j))
     return kernel_call(

time: 393 us -> 396 us (level)
  Pallas kernels: 151 us -> 156 us
    pallas_call x3, Pallas kernels: 34.3 us -> 40.1 us  [late(): kernel_call(functools.partial(late_kernel, rows), cols // tile, [whole(si...]
  transfers between devices with their start and end apart: 47 -> 47, of which waited for: 15 -> 15; matrix products, arithmetic and copies ran while one was open for 3% -> 3% of each run, Pallas kernels for 35% -> 36%
where the time goes in v3:
time: 396 us; the launch traced here: 394 us
  Pallas kernels  156 us (39%)
  waiting for transfers between devices  110 us (28%)
  starting transfers between devices  86.1 us (22%)
  blocking collectives  15.8 us (4%)
  other arithmetic  13.3 us (3%)
  local copies, waits for them, and re-layouts  11.8 us (3%)
    ppermute x30, waiting for transfers between devices, chunk_blocks(): along = lambda value, pairs: lax.ppermute(value, 'gy', pairs)  102 us
    ppermute x30, starting transfers between devices, chunk_blocks(): along = lambda value, pairs: lax.ppermute(value, 'gy', pairs)  69.1 us
    pallas_call x3, Pallas kernels, early(): kernel_call(functools.partial(early_kernel, rows), cols // tile, [whole(s...  62.9 us
    pallas_call x3, Pallas kernels, down(): kernel_call(down_kernel, 4, [whole(both, depth)] * 2 + [pl.BlockSpec((dep...  43.7 us
    pallas_call x3, Pallas kernels, late(): kernel_call(functools.partial(late_kernel, rows), cols // tile, [whole(si...  40.1 us
    all_gather x6, blocking collectives, chunk_blocks(): lax.all_gather(value, 'gx', axis_index_groups=[[0, 1], [2, 3]], axis=0, t...  15.8 us
    pallas_call x3, Pallas kernels, add_core(): kernel_call(sum_kernel, cols // tile, [piece(2, half), piece(half), piece...  8.97 us
    unnamed x30, local copies, waits for them, and re-layouts  8.6 us
  transfers between devices with their start and end apart: 47, of which 15 were waited for; matrix products, arithmetic and copies ran while one was open for 3% of the time, Pallas kernels for 36%

profile of v3, /device:TPU:0, one launch (start us, length us, event | category | flops | bytes accessed | tf_op | source)
XLA Modules:
  0.0 393.8 jit_solution(15513282214088356053)
XLA Ops:
  2.5 5.9 %collective-permute-start = (bf16[384,1152]{1,0:T(8,128)(2,1)S(1)}, bf16[384,1152]{1,0:T(8,128)(2,1)S(1)}, u32[]{:S(2)}, u32[]{:S(2)}) collective-permute-start(bf16[384,1152]{1,0:T(8,128)(2,1)S(1)} %get-tuple-element.117.own), channel_id=1, source_target_pairs={{0,1},{1,0},{2,3},{3,2},{4,5},{5,4},{6,7},{7,6},{8,9},{9,8},{10,11... | collective-permute-start | bytes 2654216 | tf_op jit(solution)/shard_map/ppermute | solution.py:198
  10.1 17.6 %collective-permute-done.pair = bf16[384,1152]{1,0:T(8,128)(2,1)S(1)} collective-permute-done((bf16[384,1152]{1,0:T(8,128)(2,1)S(1)}, bf16[384,1152]{1,0:T(8,128)(2,1)S(1)}, u32[]{:S(2)}, u32[]{:S(2)}) %collective-permute-start) | collective-permute-done | bytes 884768 | tf_op jit(solution)/shard_map/ppermute | solution.py:198
  36.6 3.5 collective-permute-start.8
  41.7 11.1 %collective-permute-done.4.outer = bf16[384,1152]{1,0:T(8,128)(2,1)S(1)} collective-permute-done((bf16[384,1152]{1,0:T(8,128)(2,1)S(1)}, bf16[384,1152]{1,0:T(8,128)(2,1)S(1)}, u32[]{:S(2)}, u32[]{:S(2)}) %collective-permute-start.4) | collective-permute-done | bytes 884768 | tf_op jit(solution)/shard_map/ppermute | solution.py:198
  62.1 21.7 %early.3.sums = f32[2,384,2304]{2,1,0:T(8,128)} custom-call(s32[5]{0:T(128)S(1)} %stack.38.at, bf16[384,1152]{1,0:T(8,128)(2,1)S(1)} %get-tuple-element.117.own, bf16[384,1152]{1,0:T(8,128)(2,1)S(1)} %copy-done.5, bf16[384,1152]{1,0:T(8,128)(2,1)S(1)} %copy-done.3, bf16[384,1152]{1,0:T(8,128)(2,1)S(1)} %copy-done.7, f32[1024,1]{1,0:T(8,128)S(1)} %copy.6.scale, ...), custom_call_target="tpu_custom_call" | custom-call | tf_op jit(solution)/shard_map/early/pallas_call | solution.py:78
  83.9 9.9 %collective-permute-done.6.outer = bf16[384,1152]{1,0:T(8,128)(2,1)} collective-permute-done((bf16[384,1152]{1,0:T(8,128)(2,1)S(1)}, bf16[384,1152]{1,0:T(8,128)(2,1)}, u32[]{:S(2)}, u32[]{:S(2)}) %collective-permute-start.6) | collective-permute-done | bytes 884768 | tf_op jit(solution)/shard_map/ppermute | solution.py:198
  93.7 14.5 %late.3 = (bf16[192,2304]{1,0:T(8,128)(2,1)S(1)}, bf16[192,2304]{1,0:T(8,128)(2,1)S(1)}, f32[2,192,2304]{2,1,0:T(8,128)}) custom-call(s32[5]{0:T(128)S(1)} %stack.38.at, bf16[384,1152]{1,0:T(8,128)(2,1)S(1)} %collective-permute-done.3.inner, bf16[384,1152]{1,0:T(8,128)(2,1)} %collective-permute-done.6.outer, f32[1024,1]{1,0:T(8,128)S(1)} %copy.6.scale, ...), custom_call_target="tpu_custom_call" | custom-call | tf_op jit(solution)/shard_map/late/pallas_call | solution.py:112
  111.9 3.5 add_core.3
  118.8 4.3 %collective-permute-start.19 = (bf16[256,1152]{1,0:T(8,128)(2,1)S(1)}, bf16[256,1152]{1,0:T(8,128)(2,1)S(1)}, u32[]{:S(2)}, u32[]{:S(2)}) collective-permute-start(bf16[256,1152]{1,0:T(8,128)(2,1)S(1)} %slice.70.own), channel_id=1, source_target_pairs={{0,1},{1,0},{2,3},{3,2},{4,5},{5,4},{6,7},{7,6},{8,9},{9,8},{10,11... | collective-permute-start | bytes 1769480 | tf_op jit(solution)/shard_map/ppermute | solution.py:198
  123.0 11.0 %collective-permute-done.16.outer = bf16[384,1152]{1,0:T(8,128)(2,1)S(1)} collective-permute-done((bf16[384,1152]{1,0:T(8,128)(2,1)}, bf16[384,1152]{1,0:T(8,128)(2,1)S(1)}, u32[]{:S(2)}, u32[]{:S(2)}) %collective-permute-start.16) | collective-permute-done | bytes 884768 | tf_op jit(solution)/shard_map/ppermute | solution.py:198
  135.3 22.3 %early.4.sums = f32[2,384,2304]{2,1,0:T(8,128)} custom-call(s32[5]{0:T(128)S(1)} %stack.38.at, bf16[384,1152]{1,0:T(8,128)(2,1)S(1)} %get-tuple-element.136.own, bf16[384,1152]{1,0:T(8,128)(2,1)} %collective-permute-done.10.pair, bf16[384,1152]{1,0:T(8,128)(2,1)} %collective-permute-done.11.inner, bf16[384,1152]{1,0:T(8,128)(2,1)S(1)} %collective-permute-done.16.outer, ...), custom_call_target="tpu_custom_call" | custom-call | tf_op jit(solution)/shard_map/early/pallas_call | solution.py:78
  164.7 14.0 %late.4 = (bf16[192,2304]{1,0:T(8,128)(2,1)S(1)}, bf16[192,2304]{1,0:T(8,128)(2,1)S(1)}, f32[2,192,2304]{2,1,0:T(8,128)}) custom-call(s32[5]{0:T(128)S(1)} %stack.38.at, bf16[384,1152]{1,0:T(8,128)(2,1)S(1)} %collective-permute-done.15.inner, bf16[384,1152]{1,0:T(8,128)(2,1)S(1)} %collective-permute-done.18.outer, f32[1024,1]{1,0:T(8,128)S(1)} %copy.6.scale, ...), custom_call_target="tpu_custom_call" | custom-call | tf_op jit(solution)/shard_map/late/pallas_call | solution.py:112
  179.2 3.8 all_gather.18.near
  185.6 15.5 %down.3 = (f32[4,384,1152]{2,1,0:T(8,128)}, bf16[384,1152]{1,0:T(8,128)(2,1)}) custom-call(s32[5]{0:T(128)S(1)} %stack.38.at, bf16[192,2304]{1,0:T(8,128)(2,1)S(1)} %all_gather.18.near, bf16[192,2304]{1,0:T(8,128)(2,1)S(1)} %all_gather.19.far, bf16[2304,4608]{1,0:T(8,128)(2,1)} %weight.5), custom_call_target="tpu_custom_call" | custom-call | tf_op jit(solution)/shard_map/down/pallas_call | solution.py:170
  201.1 5.0 %collective-permute-start.21 = (bf16[384,1152]{1,0:T(8,128)(2,1)}, bf16[384,1152]{1,0:T(8,128)(2,1)}, u32[]{:S(2)}, u32[]{:S(2)}) collective-permute-start(bf16[384,1152]{1,0:T(8,128)(2,1)} %get-tuple-element.152), channel_id=1, source_target_pairs={{0,1},{3,2},{4,5},{7,6},{8,9},{11,10},{12,13},{15,14},{16,17},{19,... | collective-permute-start | bytes 2654216 | tf_op jit(solution)/shard_map/ppermute | solution.py:198
  206.2 4.3 %add_core.4 = (bf16[2,96,2304]{2,1,0:T(8,128)(2,1)}, f32[2,96,2304]{2,1,0:T(8,128)S(1)}) custom-call(s32[5]{0:T(128)S(1)} %stack.38.at, f32[2,192,2304]{2,1,0:T(8,128)} %get-tuple-element.155.keep, bf16[192,2304]{1,0:T(8,128)(2,1)S(1)} %collective-permute-done.24.gate, bf16[192,2304]{1,0:T(8,128)(2,1)S(1)} %collective-permute-done.25.up), custom_call_target="tpu_custom_call" | custom-call | tf_op jit(solution)/shard_map/add_core/pallas_call | solution.py:137
  214.6 18.9 %early.5.sums = f32[2,256,2304]{2,1,0:T(8,128)} custom-call(s32[5]{0:T(128)S(1)} %stack.38.at, bf16[256,1152]{1,0:T(8,128)(2,1)S(1)} %slice.70.own, bf16[256,1152]{1,0:T(8,128)(2,1)S(1)} %collective-permute-done.19.pair, bf16[256,1152]{1,0:T(8,128)(2,1)S(1)} %collective-permute-done.20.inner, bf16[256,1152]{1,0:T(8,128)(2,1)S(1)} %copy-done.9, ...), custom_call_target="tpu_custom_call" | custom-call | tf_op jit(solution)/shard_map/early/pallas_call | solution.py:78
  236.3 7.3 %collective-permute-start.26 = (bf16[384,1152]{1,0:T(8,128)(2,1)S(1)}, bf16[384,1152]{1,0:T(8,128)(2,1)S(1)}, u32[]{:S(2)}, u32[]{:S(2)}) collective-permute-start(bf16[384,1152]{1,0:T(8,128)(2,1)S(1)} %fusion.6), channel_id=1, source_target_pairs={{0,1},{3,2},{4,5},{7,6},{8,9},{11,10},{12,13},{15,14},{16,17},{19,... | collective-permute-start | bytes 2654216 | tf_op jit(solution)/shard_map/ppermute | solution.py:198
  243.6 11.7 %late.5 = (bf16[128,2304]{1,0:T(8,128)(2,1)S(1)}, bf16[128,2304]{1,0:T(8,128)(2,1)S(1)}, f32[2,128,2304]{2,1,0:T(8,128)S(1)}) custom-call(s32[5]{0:T(128)S(1)} %stack.38.at, bf16[256,1152]{1,0:T(8,128)(2,1)} %collective-permute-done.22.inner, bf16[256,1152]{1,0:T(8,128)(2,1)} %collective-permute-done.28.outer, f32[1024,1]{1,0:T(8,128)S(1)} %copy.6.scale, ...), custom_call_target="tpu_custom_call" | custom-call | tf_op jit(solution)/shard_map/late/pallas_call | solution.py:112
  266.4 3.4 collective-permute-start.32
  273.0 15.2 %down.4 = (f32[4,384,1152]{2,1,0:T(8,128)}, bf16[384,1152]{1,0:T(8,128)(2,1)S(1)}) custom-call(s32[5]{0:T(128)S(1)} %stack.38.at, bf16[192,2304]{1,0:T(8,128)(2,1)S(1)} %all_gather.20.near, bf16[192,2304]{1,0:T(8,128)(2,1)S(1)} %all_gather.21.far, bf16[2304,4608]{1,0:T(8,128)(2,1)} %weight.5), custom_call_target="tpu_custom_call" | custom-call | tf_op jit(solution)/shard_map/down/pallas_call | solution.py:170
  295.3 3.6 collective-permute-done.37
  301.3 13.1 %down.5 = (f32[4,256,1152]{2,1,0:T(8,128)}, bf16[256,1152]{1,0:T(8,128)(2,1)S(1)}) custom-call(s32[5]{0:T(128)S(1)} %stack.38.at, bf16[128,2304]{1,0:T(8,128)(2,1)S(1)} %all_gather.22.near, bf16[128,2304]{1,0:T(8,128)(2,1)S(1)} %all_gather.23.far, bf16[2304,4608]{1,0:T(8,128)(2,1)} %weight.5), custom_call_target="tpu_custom_call" | custom-call | tf_op jit(solution)/shard_map/down/pallas_call | solution.py:170
  316.7 3.7 collective-permute-start.38
  320.4 8.9 %collective-permute-done.40 = bf16[256,1152]{1,0:T(8,128)(2,1)S(1)} collective-permute-done((bf16[256,1152]{1,0:T(8,128)(2,1)S(1)}, bf16[256,1152]{1,0:T(8,128)(2,1)S(1)}, u32[]{:S(2)}, u32[]{:S(2)}) %collective-permute-start.40) | collective-permute-done | bytes 589856 | tf_op jit(solution)/shard_map/ppermute | solution.py:198
  331.5 7.1 %collective-permute-start.43 = (bf16[256,1152]{1,0:T(8,128)(2,1)S(1)}, bf16[256,1152]{1,0:T(8,128)(2,1)S(1)}, u32[]{:S(2)}, u32[]{:S(2)}) collective-permute-start(bf16[256,1152]{1,0:T(8,128)(2,1)S(1)} %fusion.14), channel_id=1, source_target_pairs={{0,1},{3,2},{4,5},{7,6},{8,9},{11,10},{12,13},{15,14},{16,17},{19,... | collective-permute-start | bytes 1769480 | tf_op jit(solution)/shard_map/ppermute | solution.py:198
  338.7 9.6 %collective-permute-done.38 = bf16[384,1152]{1,0:T(8,128)(2,1)S(1)} collective-permute-done((bf16[384,1152]{1,0:T(8,128)(2,1)S(1)}, bf16[384,1152]{1,0:T(8,128)(2,1)S(1)}, u32[]{:S(2)}, u32[]{:S(2)}) %collective-permute-start.38) | collective-permute-done | bytes 884768 | tf_op jit(solution)/shard_map/ppermute | solution.py:198
  349.3 5.1 %collective-permute-start.41 = (bf16[384,1152]{1,0:T(8,128)(2,1)S(1)}, bf16[384,1152]{1,0:T(8,128)(2,1)S(1)}, u32[]{:S(2)}, u32[]{:S(2)}) collective-permute-start(bf16[384,1152]{1,0:T(8,128)(2,1)S(1)} %get-tuple-element.202), channel_id=1, source_target_pairs={{0,1},{1,0},{2,3},{3,2},{4,5},{5,4},{6,7},{7,6},{8,9},{9,8},{10,11... | collective-permute-start | bytes 2654216 | tf_op jit(solution)/shard_map/ppermute | solution.py:198
  354.4 6.5 %collective-permute-done.43 = bf16[256,1152]{1,0:T(8,128)(2,1)S(1)} collective-permute-done((bf16[256,1152]{1,0:T(8,128)(2,1)S(1)}, bf16[256,1152]{1,0:T(8,128)(2,1)S(1)}, u32[]{:S(2)}, u32[]{:S(2)}) %collective-permute-start.43) | collective-permute-done | bytes 589856 | tf_op jit(solution)/shard_map/ppermute | solution.py:198
  361.8 5.1 %collective-permute-start.45 = (bf16[256,1152]{1,0:T(8,128)(2,1)S(1)}, bf16[256,1152]{1,0:T(8,128)(2,1)S(1)}, u32[]{:S(2)}, u32[]{:S(2)}) collective-permute-start(bf16[256,1152]{1,0:T(8,128)(2,1)S(1)} %get-tuple-element.206), channel_id=1, source_target_pairs={{0,1},{1,0},{2,3},{3,2},{4,5},{5,4},{6,7},{7,6},{8,9},{9,8},{10,11... | collective-permute-start | bytes 1769480 | tf_op jit(solution)/shard_map/ppermute | solution.py:198
  366.9 12.9 %collective-permute-done.41 = bf16[384,1152]{1,0:T(8,128)(2,1)S(1)} collective-permute-done((bf16[384,1152]{1,0:T(8,128)(2,1)S(1)}, bf16[384,1152]{1,0:T(8,128)(2,1)S(1)}, u32[]{:S(2)}, u32[]{:S(2)}) %collective-permute-start.41) | collective-permute-done | bytes 884768 | tf_op jit(solution)/shard_map/ppermute | solution.py:198
  380.2 11.8 %collective-permute-done.45 = bf16[256,1152]{1,0:T(8,128)(2,1)S(1)} collective-permute-done((bf16[256,1152]{1,0:T(8,128)(2,1)S(1)}, bf16[256,1152]{1,0:T(8,128)(2,1)S(1)}, u32[]{:S(2)}, u32[]{:S(2)}) %collective-permute-start.45) | collective-permute-done | bytes 589856 | tf_op jit(solution)/shard_map/ppermute | solution.py:198
  (146 shorter events, 81.5 us)
Async XLA Ops:
  2.5 25.2 %collective-permute-start = (bf16[384,1152]{1,0:T(8,128)(2,1)S(1)}, bf16[384,1152]{1,0:T(8,128)(2,1)S(1)}, u32[]{:S(2)}, u32[]{:S(2)}) collective-permute-start(bf16[384,1152]{1,0:T(8,128)(2,1)S(1)} %get-tuple-element.117.own), channel_id=1, source_target_pairs={{0,1},{1,0},{2,3},{3,2},{4,5},{5,4},{6,7},{7,6},{8,9},{9,8},{10,11... | collective-permute-start | bytes 2654216 | tf_op jit(solution)/shard_map/ppermute | solution.py:198
  29.3 23.5 %collective-permute-start.4 = (bf16[384,1152]{1,0:T(8,128)(2,1)S(1)}, bf16[384,1152]{1,0:T(8,128)(2,1)S(1)}, u32[]{:S(2)}, u32[]{:S(2)}) collective-permute-start(bf16[384,1152]{1,0:T(8,128)(2,1)S(1)} %collective-permute-done.1.inner), channel_id=1, source_target_pairs={{1,0},{2,3},{5,4},{6,7},{9,8},{10,11},{13,12},{14,15},{17,16},{18,... | collective-permute-start | bytes 2654216 | tf_op jit(solution)/shard_map/ppermute | solution.py:198
  35.2 18.6 %collective-permute-start.9 = (f32[2176]{0:T(1024)S(1)}, f32[2176]{0:T(1024)S(1)}, u32[]{:S(2)}, u32[]{:S(2)}) collective-permute-start(f32[2176]{0:T(1024)S(1)} %pad_maximum_fusion.2), channel_id=1, source_target_pairs={{0,3},{1,0},{2,1},{3,2},{4,7},{5,4},{6,5},{7,6},{8,11},{9,8},{10,9... | collective-permute-start | bytes 26120 | tf_op jit(solution)/shard_map/ppermute | solution.py:271
  53.9 29.9 %collective-permute-start.11 = (bf16[384,1152]{1,0:T(8,128)(2,1)S(1)}, bf16[384,1152]{1,0:T(8,128)(2,1)}, u32[]{:S(2)}, u32[]{:S(2)}) collective-permute-start(bf16[384,1152]{1,0:T(8,128)(2,1)S(1)} %get-tuple-element.136.own), channel_id=1, source_target_pairs={{1,2},{2,1},{5,6},{6,5},{9,10},{10,9},{13,14},{14,13},{17,18},{18,... | collective-permute-start | bytes 2654216 | tf_op jit(solution)/shard_map/ppermute | solution.py:198
  55.6 28.3 %collective-permute-start.10 = (bf16[384,1152]{1,0:T(8,128)(2,1)S(1)}, bf16[384,1152]{1,0:T(8,128)(2,1)}, u32[]{:S(2)}, u32[]{:S(2)}) collective-permute-start(bf16[384,1152]{1,0:T(8,128)(2,1)S(1)} %get-tuple-element.136.own), channel_id=1, source_target_pairs={{0,1},{1,0},{2,3},{3,2},{4,5},{5,4},{6,7},{7,6},{8,9},{9,8},{10,11... | collective-permute-start | bytes 2654216 | tf_op jit(solution)/shard_map/ppermute | solution.py:198
  57.0 36.8 %collective-permute-start.6 = (bf16[384,1152]{1,0:T(8,128)(2,1)S(1)}, bf16[384,1152]{1,0:T(8,128)(2,1)}, u32[]{:S(2)}, u32[]{:S(2)}) collective-permute-start(bf16[384,1152]{1,0:T(8,128)(2,1)S(1)} %collective-permute-done.3.inner), channel_id=1, source_target_pairs={{1,0},{2,3},{5,4},{6,7},{9,8},{10,11},{13,12},{14,15},{17,16},{18,... | collective-permute-start | bytes 2654216 | tf_op jit(solution)/shard_map/ppermute | solution.py:198
  109.4 24.6 %collective-permute-start.16 = (bf16[384,1152]{1,0:T(8,128)(2,1)}, bf16[384,1152]{1,0:T(8,128)(2,1)S(1)}, u32[]{:S(2)}, u32[]{:S(2)}) collective-permute-start(bf16[384,1152]{1,0:T(8,128)(2,1)} %collective-permute-done.11.inner), channel_id=1, source_target_pairs={{1,0},{2,3},{5,4},{6,7},{9,8},{10,11},{13,12},{14,15},{17,16},{18,... | collective-permute-start | bytes 2654216 | tf_op jit(solution)/shard_map/ppermute | solution.py:198
  115.4 42.2 %collective-permute-start.14 = (bf16[2,96,2304]{2,1,0:T(8,128)(2,1)S(1)}, bf16[2,96,2304]{2,1,0:T(8,128)(2,1)S(1)}, u32[]{:S(2)}, u32[]{:S(2)}) collective-permute-start(bf16[2,96,2304]{2,1,0:T(8,128)(2,1)S(1)} %get-tuple-element.131), channel_id=1, source_target_pairs={{0,8},{4,12},{8,0},{12,4},{1,9},{5,13},{9,1},{13,5},{2,10},{6,14},... | collective-permute-start | bytes 2654216 | tf_op jit(solution)/shard_map/ppermute | solution.py:222
  118.1 41.5 %collective-permute-start.20 = (bf16[256,1152]{1,0:T(8,128)(2,1)S(1)}, bf16[256,1152]{1,0:T(8,128)(2,1)S(1)}, u32[]{:S(2)}, u32[]{:S(2)}) collective-permute-start(bf16[256,1152]{1,0:T(8,128)(2,1)S(1)} %slice.70.own), channel_id=1, source_target_pairs={{1,2},{2,1},{5,6},{6,5},{9,10},{10,9},{13,14},{14,13},{17,18},{18,... | collective-permute-start | bytes 1769480 | tf_op jit(solution)/shard_map/ppermute | solution.py:198
  118.8 40.8 %collective-permute-start.19 = (bf16[256,1152]{1,0:T(8,128)(2,1)S(1)}, bf16[256,1152]{1,0:T(8,128)(2,1)S(1)}, u32[]{:S(2)}, u32[]{:S(2)}) collective-permute-start(bf16[256,1152]{1,0:T(8,128)(2,1)S(1)} %slice.70.own), channel_id=1, source_target_pairs={{0,1},{1,0},{2,3},{3,2},{4,5},{5,4},{6,7},{7,6},{8,9},{9,8},{10,11... | collective-permute-start | bytes 1769480 | tf_op jit(solution)/shard_map/ppermute | solution.py:198
  134.1 30.6 %collective-permute-start.18 = (bf16[384,1152]{1,0:T(8,128)(2,1)S(1)}, bf16[384,1152]{1,0:T(8,128)(2,1)S(1)}, u32[]{:S(2)}, u32[]{:S(2)}) collective-permute-start(bf16[384,1152]{1,0:T(8,128)(2,1)S(1)} %collective-permute-done.15.inner), channel_id=1, source_target_pairs={{1,0},{2,3},{5,4},{6,7},{9,8},{10,11},{13,12},{14,15},{17,16},{18,... | collective-permute-start | bytes 2654216 | tf_op jit(solution)/shard_map/ppermute | solution.py:198
  158.0 25.0 %collective-permute-start.17 = (bf16[96,2304]{1,0:T(8,128)(2,1)S(1)}, bf16[96,2304]{1,0:T(8,128)(2,1)S(1)}, u32[]{:S(2)}, u32[]{:S(2)}) collective-permute-start(bf16[96,2304]{1,0:T(8,128)(2,1)S(1)} %fusion.18), channel_id=1, source_target_pairs={{0,8},{4,12},{8,0},{12,4},{1,9},{5,13},{9,1},{13,5},{2,10},{6,14},... | collective-permute-start | bytes 1327112 | tf_op jit(solution)/shard_map/ppermute | solution.py:229
  159.6 46.6 %collective-permute-start.22 = (bf16[256,1152]{1,0:T(8,128)(2,1)S(1)}, bf16[256,1152]{1,0:T(8,128)(2,1)}, u32[]{:S(2)}, u32[]{:S(2)}) collective-permute-start(bf16[256,1152]{1,0:T(8,128)(2,1)S(1)} %collective-permute-done.19.pair), channel_id=1, source_target_pairs={{1,2},{2,1},{5,6},{6,5},{9,10},{10,9},{13,14},{14,13},{17,18},{18,... | collective-permute-start | bytes 1769480 | tf_op jit(solution)/shard_map/ppermute | solution.py:198
  161.1 45.1 %collective-permute-start.23 = (bf16[256,1152]{1,0:T(8,128)(2,1)S(1)}, bf16[256,1152]{1,0:T(8,128)(2,1)S(1)}, u32[]{:S(2)}, u32[]{:S(2)}) collective-permute-start(bf16[256,1152]{1,0:T(8,128)(2,1)S(1)} %collective-permute-done.20.inner), channel_id=1, source_target_pairs={{1,0},{2,3},{5,4},{6,7},{9,8},{10,11},{13,12},{14,15},{17,16},{18,... | collective-permute-start | bytes 1769480 | tf_op jit(solution)/shard_map/ppermute | solution.py:198
  178.7 27.5 %collective-permute-start.24 = (bf16[192,2304]{1,0:T(8,128)(2,1)S(1)}, bf16[192,2304]{1,0:T(8,128)(2,1)S(1)}, u32[]{:S(2)}, u32[]{:S(2)}) collective-permute-start(bf16[192,2304]{1,0:T(8,128)(2,1)S(1)} %get-tuple-element.146), channel_id=1, source_target_pairs={{0,4},{4,0},{8,12},{12,8},{1,5},{5,1},{9,13},{13,9},{2,6},{6,2},{1... | collective-permute-start | bytes 2654216 | tf_op jit(solution)/shard_map/ppermute | solution.py:217
  178.7 27.5 %collective-permute-start.25 = (bf16[192,2304]{1,0:T(8,128)(2,1)S(1)}, bf16[192,2304]{1,0:T(8,128)(2,1)S(1)}, u32[]{:S(2)}, u32[]{:S(2)}) collective-permute-start(bf16[192,2304]{1,0:T(8,128)(2,1)S(1)} %get-tuple-element.147), channel_id=1, source_target_pairs={{0,4},{4,0},{8,12},{12,8},{1,5},{5,1},{9,13},{13,9},{2,6},{6,2},{1... | collective-permute-start | bytes 2654216 | tf_op jit(solution)/shard_map/ppermute | solution.py:217
  201.1 32.4 %collective-permute-start.21 = (bf16[384,1152]{1,0:T(8,128)(2,1)}, bf16[384,1152]{1,0:T(8,128)(2,1)}, u32[]{:S(2)}, u32[]{:S(2)}) collective-permute-start(bf16[384,1152]{1,0:T(8,128)(2,1)} %get-tuple-element.152), channel_id=1, source_target_pairs={{0,1},{3,2},{4,5},{7,6},{8,9},{11,10},{12,13},{15,14},{16,17},{19,... | collective-permute-start | bytes 2654216 | tf_op jit(solution)/shard_map/ppermute | solution.py:198
  211.7 44.2 %collective-permute-start.31 = (bf16[2,96,2304]{2,1,0:T(8,128)(2,1)}, bf16[2,96,2304]{2,1,0:T(8,128)(2,1)}, u32[]{:S(2)}, u32[]{:S(2)}) collective-permute-start(bf16[2,96,2304]{2,1,0:T(8,128)(2,1)} %get-tuple-element.158), channel_id=1, source_target_pairs={{0,8},{4,12},{8,0},{12,4},{1,9},{5,13},{9,1},{13,5},{2,10},{6,14},... | collective-permute-start | bytes 2654216 | tf_op jit(solution)/shard_map/ppermute | solution.py:222
  212.2 31.4 %collective-permute-start.28 = (bf16[256,1152]{1,0:T(8,128)(2,1)}, bf16[256,1152]{1,0:T(8,128)(2,1)}, u32[]{:S(2)}, u32[]{:S(2)}) collective-permute-start(bf16[256,1152]{1,0:T(8,128)(2,1)} %collective-permute-done.22.inner), channel_id=1, source_target_pairs={{1,0},{2,3},{5,4},{6,7},{9,8},{10,11},{13,12},{14,15},{17,16},{18,... | collective-permute-start | bytes 1769480 | tf_op jit(solution)/shard_map/ppermute | solution.py:198
  235.5 27.8 %collective-permute-start.27 = (bf16[384,1152]{1,0:T(8,128)(2,1)S(1)}, bf16[384,1152]{1,0:T(8,128)(2,1)S(1)}, u32[]{:S(2)}, u32[]{:S(2)}) collective-permute-start(bf16[384,1152]{1,0:T(8,128)(2,1)S(1)} %fusion.6), channel_id=1, source_target_pairs={{1,2},{2,1},{5,6},{6,5},{9,10},{10,9},{13,14},{14,13},{17,18},{18,... | collective-permute-start | bytes 2654216 | tf_op jit(solution)/shard_map/ppermute | solution.py:198
  236.3 26.9 %collective-permute-start.26 = (bf16[384,1152]{1,0:T(8,128)(2,1)S(1)}, bf16[384,1152]{1,0:T(8,128)(2,1)S(1)}, u32[]{:S(2)}, u32[]{:S(2)}) collective-permute-start(bf16[384,1152]{1,0:T(8,128)(2,1)S(1)} %fusion.6), channel_id=1, source_target_pairs={{0,1},{3,2},{4,5},{7,6},{8,9},{11,10},{12,13},{15,14},{16,17},{19,... | collective-permute-start | bytes 2654216 | tf_op jit(solution)/shard_map/ppermute | solution.py:198
  262.6 26.9 %collective-permute-start.34 = (bf16[2,64,2304]{2,1,0:T(8,128)(2,1)S(1)}, bf16[2,64,2304]{2,1,0:T(8,128)(2,1)S(1)}, u32[]{:S(2)}, u32[]{:S(2)}) collective-permute-start(bf16[2,64,2304]{2,1,0:T(8,128)(2,1)S(1)} %get-tuple-element.175), channel_id=1, source_target_pairs={{0,8},{4,12},{8,0},{12,4},{1,9},{5,13},{9,1},{13,5},{2,10},{6,14},... | collective-permute-start | bytes 1769480 | tf_op jit(solution)/shard_map/ppermute | solution.py:222
  265.7 27.8 %collective-permute-start.33 = (bf16[384,1152]{1,0:T(8,128)(2,1)S(1)}, bf16[384,1152]{1,0:T(8,128)(2,1)S(1)}, u32[]{:S(2)}, u32[]{:S(2)}) collective-permute-start(bf16[384,1152]{1,0:T(8,128)(2,1)S(1)} %get-tuple-element.203), channel_id=1, source_target_pairs={{1,2},{2,1},{5,6},{6,5},{9,10},{10,9},{13,14},{14,13},{17,18},{18,... | collective-permute-start | bytes 2654216 | tf_op jit(solution)/shard_map/ppermute | solution.py:198
  266.4 27.1 %collective-permute-start.32 = (bf16[384,1152]{1,0:T(8,128)(2,1)S(1)}, bf16[384,1152]{1,0:T(8,128)(2,1)S(1)}, u32[]{:S(2)}, u32[]{:S(2)}) collective-permute-start(bf16[384,1152]{1,0:T(8,128)(2,1)S(1)} %get-tuple-element.204), channel_id=1, source_target_pairs={{0,1},{1,0},{2,3},{3,2},{4,5},{5,4},{6,7},{7,6},{8,9},{9,8},{10,11... | collective-permute-start | bytes 2654216 | tf_op jit(solution)/shard_map/ppermute | solution.py:198
  288.2 27.5 %collective-permute-start.36 = (bf16[384,1152]{1,0:T(8,128)(2,1)S(1)}, bf16[384,1152]{1,0:T(8,128)(2,1)S(1)}, u32[]{:S(2)}, u32[]{:S(2)}) collective-permute-start(bf16[384,1152]{1,0:T(8,128)(2,1)S(1)} %get-tuple-element.181), channel_id=1, source_target_pairs={{0,1},{3,2},{4,5},{7,6},{8,9},{11,10},{12,13},{15,14},{16,17},{19,... | collective-permute-start | bytes 2654216 | tf_op jit(solution)/shard_map/ppermute | solution.py:198
  315.9 22.7 %collective-permute-start.39 = (bf16[384,1152]{1,0:T(8,128)(2,1)S(1)}, bf16[384,1152]{1,0:T(8,128)(2,1)S(1)}, u32[]{:S(2)}, u32[]{:S(2)}) collective-permute-start(bf16[384,1152]{1,0:T(8,128)(2,1)S(1)} %fusion.1), channel_id=1, source_target_pairs={{1,2},{2,1},{5,6},{6,5},{9,10},{10,9},{13,14},{14,13},{17,18},{18,... | collective-permute-start | bytes 2654216 | tf_op jit(solution)/shard_map/ppermute | solution.py:198
  316.7 31.6 %collective-permute-start.38 = (bf16[384,1152]{1,0:T(8,128)(2,1)S(1)}, bf16[384,1152]{1,0:T(8,128)(2,1)S(1)}, u32[]{:S(2)}, u32[]{:S(2)}) collective-permute-start(bf16[384,1152]{1,0:T(8,128)(2,1)S(1)} %fusion.1), channel_id=1, source_target_pairs={{0,1},{3,2},{4,5},{7,6},{8,9},{11,10},{12,13},{15,14},{16,17},{19,... | collective-permute-start | bytes 2654216 | tf_op jit(solution)/shard_map/ppermute | solution.py:198
  330.7 23.7 %collective-permute-start.44 = (bf16[256,1152]{1,0:T(8,128)(2,1)S(1)}, bf16[256,1152]{1,0:T(8,128)(2,1)S(1)}, u32[]{:S(2)}, u32[]{:S(2)}) collective-permute-start(bf16[256,1152]{1,0:T(8,128)(2,1)S(1)} %fusion.14), channel_id=1, source_target_pairs={{1,2},{2,1},{5,6},{6,5},{9,10},{10,9},{13,14},{14,13},{17,18},{18,... | collective-permute-start | bytes 1769480 | tf_op jit(solution)/shard_map/ppermute | solution.py:198
  331.5 29.4 %collective-permute-start.43 = (bf16[256,1152]{1,0:T(8,128)(2,1)S(1)}, bf16[256,1152]{1,0:T(8,128)(2,1)S(1)}, u32[]{:S(2)}, u32[]{:S(2)}) collective-permute-start(bf16[256,1152]{1,0:T(8,128)(2,1)S(1)} %fusion.14), channel_id=1, source_target_pairs={{0,1},{3,2},{4,5},{7,6},{8,9},{11,10},{12,13},{15,14},{16,17},{19,... | collective-permute-start | bytes 1769480 | tf_op jit(solution)/shard_map/ppermute | solution.py:198
  349.3 30.5 %collective-permute-start.41 = (bf16[384,1152]{1,0:T(8,128)(2,1)S(1)}, bf16[384,1152]{1,0:T(8,128)(2,1)S(1)}, u32[]{:S(2)}, u32[]{:S(2)}) collective-permute-start(bf16[384,1152]{1,0:T(8,128)(2,1)S(1)} %get-tuple-element.202), channel_id=1, source_target_pairs={{0,1},{1,0},{2,3},{3,2},{4,5},{5,4},{6,7},{7,6},{8,9},{9,8},{10,11... | collective-permute-start | bytes 2654216 | tf_op jit(solution)/shard_map/ppermute | solution.py:198
  361.1 19.1 %collective-permute-start.46 = (bf16[256,1152]{1,0:T(8,128)(2,1)S(1)}, bf16[256,1152]{1,0:T(8,128)(2,1)S(1)}, u32[]{:S(2)}, u32[]{:S(2)}) collective-permute-start(bf16[256,1152]{1,0:T(8,128)(2,1)S(1)} %get-tuple-element.205), channel_id=1, source_target_pairs={{1,2},{2,1},{5,6},{6,5},{9,10},{10,9},{13,14},{14,13},{17,18},{18,... | collective-permute-start | bytes 1769480 | tf_op jit(solution)/shard_map/ppermute | solution.py:198
  361.8 30.2 %collective-permute-start.45 = (bf16[256,1152]{1,0:T(8,128)(2,1)S(1)}, bf16[256,1152]{1,0:T(8,128)(2,1)S(1)}, u32[]{:S(2)}, u32[]{:S(2)}) collective-permute-start(bf16[256,1152]{1,0:T(8,128)(2,1)S(1)} %get-tuple-element.206), channel_id=1, source_target_pairs={{0,1},{1,0},{2,3},{3,2},{4,5},{5,4},{6,7},{7,6},{8,9},{9,8},{10,11... | collective-permute-start | bytes 1769480 | tf_op jit(solution)/shard_map/ppermute | solution.py:198
  (30 other events, 280.7 us)
